TPU v7x, 128 devices: a whole 4x4x4 slice. The times are simulated.
128 devices in a mesh: bx: 8 (over y_lo, z), by: 16 (over y_hi, x, core).
Axes of the slice: x: 4, y: 4 (y_hi: 2, y_lo: 2; y = y_hi * 2 + y_lo), z: 4, core: 2. Of those that a mesh axis runs over, the one named last changes fastest.
Arguments:
- populations: float32 [19, 256, 512, 128], P(None, 'bx', 'by'), may hold values from 0.2 to 8, as said below
- fluid_mask: int32 [256, 512, 128], P('bx', 'by'), may hold values from 0 to 1, as said below
- rate_class: int32 [256, 512, 128], P('bx', 'by'), may hold values from 0 to 3
- class_rates: float32 [4], replicated, may hold values from 0.6 to 1.8
Outputs:
- final_populations: float32 [19, 256, 512, 128], P(None, 'bx', 'by')
- mean_flow: float32 [1], replicated
Inputs may be any that keep to these rules, and one draw needn't show every extreme that they name: `fluid_mask`: at least one cell is fluid. `populations`: every population is positive.
All inputs are finite; a program needn't handle non-finite values.
Results may differ from a plain program's by a relative error of at most 0.00002.
Values sent between devices are 32-bit elements; how exact they have to be, the bound alone decides.
No kernel may reach another device: no remote copies, remote signals or barrier semaphores. Data moves between devices by JAX's collectives and lax.ppermute only.
A program may use at most 192 MiB of HBM per device.

v0:
```python
import jax
import jax.numpy as jnp
from jax import lax
from jax.experimental import pallas as pl
from jax.experimental.pallas import tpu as pltpu
from jax.sharding import PartitionSpec as P

VELOCITY = [
    (0, 0, 0),
    (1, 0, 0),
    (-1, 0, 0),
    (0, 1, 0),
    (0, -1, 0),
    (0, 0, 1),
    (0, 0, -1),
    (1, 1, 0),
    (-1, -1, 0),
    (1, -1, 0),
    (-1, 1, 0),
    (1, 0, 1),
    (-1, 0, -1),
    (1, 0, -1),
    (-1, 0, 1),
    (0, 1, 1),
    (0, -1, -1),
    (0, 1, -1),
    (0, -1, 1),
]
OPPOSITE = [0, 2, 1, 4, 3, 6, 5, 8, 7, 10, 9, 12, 11, 14, 13, 16, 15, 18, 17]
UP_X = [q for q in range(19) if VELOCITY[q][0] == 1]
DOWN_X = [OPPOSITE[q] for q in UP_X]
UP_Y = [q for q in range(19) if VELOCITY[q][1] == 1]
DOWN_Y = [OPPOSITE[q] for q in UP_Y]
CORNERS = [(7, 1, 1), (8, -1, -1), (9, 1, -1), (10, -1, 1)]

OFF = 8
F32 = jnp.float32
MIB = 1024 * 1024


def collide(f, rate):
    plus = {}
    diff = {}
    for q in range(1, 19, 2):
        plus[q] = f[q] + f[q + 1]
        diff[q] = f[q] - f[q + 1]
    rho = ((f[0] + plus[1]) + (plus[3] + plus[5])) + (
        ((plus[7] + plus[9]) + (plus[11] + plus[13])) + (plus[15] + plus[17])
    )
    mx = (diff[1] + diff[7]) + (diff[9] + diff[11]) + diff[13]
    my = (diff[3] + diff[7]) + (diff[15] - diff[9]) + diff[17]
    mz = (diff[5] + diff[11]) + (diff[15] - diff[13]) - diff[17]
    inv = 4.5 / rho
    ux = inv * mx
    uy = inv * my
    uz = inv * mz
    tx = ux * mx
    ty = uy * my
    tz = uz * mz
    base = rho - ((tx + ty) + tz) * (1.0 / 3.0)
    keep = 1.0 - rate
    r36 = rate * (1.0 / 36.0)
    r18 = rate * (1.0 / 18.0)
    r12 = rate * (1.0 / 12.0)
    gx = r12 * mx
    gy = r12 * my
    gz = r12 * mz
    ux2 = ux + ux
    uy2 = uy + uy
    cross = {7: ux2 * my, 11: ux2 * mz, 15: uy2 * mz}
    pair_base = {7: base + (tx + ty), 11: base + (tx + tz), 15: base + (ty + tz)}
    lean = {7: (gx, gy), 11: (gx, gz), 15: (gy, gz)}
    out = [None] * 19
    out[0] = keep * f[0] + (rate * (1.0 / 3.0)) * base
    for q, t, g in ((1, tx, gx), (3, ty, gy), (5, tz, gz)):
        even = r18 * (base + t)
        odd = g + g
        out[q] = keep * f[q] + (even + odd)
        out[q + 1] = keep * f[q + 1] + (even - odd)
    for q in (7, 11, 15):
        one, two = lean[q]
        even = r36 * (pair_base[q] + cross[q])
        odd = one + two
        out[q] = keep * f[q] + (even + odd)
        out[q + 1] = keep * f[q + 1] + (even - odd)
        even = r36 * (pair_base[q] - cross[q])
        odd = one - two
        out[q + 2] = keep * f[q + 2] + (even + odd)
        out[q + 3] = keep * f[q + 3] + (even - odd)
    return out, mz


def turn(value, step):
    if step == 0:
        return value
    return pltpu.roll(value, step % value.shape[-1], axis=value.ndim - 1)


def cell_rate(cls, fluid, rates):
    rate = jnp.where(cls == 0, rates[0], rates[1])
    rate = jnp.where(cls == 2, rates[2], rate)
    rate = jnp.where(cls == 3, rates[3], rate)
    return jnp.where(fluid, rate, 0.0)


def pull(local, load, is_open):
    out = [local[0]]
    links = [None]
    for q in range(1, 19):
        move = VELOCITY[q]
        source = local[q] if move[0] == 0 and move[1] == 0 else load(q, move[0], move[1])
        links.append(is_open(q))
        out.append(jnp.where(links[q], turn(source, move[2]), local[OPPOSITE[q]]))
    return out, links


def open_by_flag(load_flag, fluid):
    limit = jnp.where(fluid > 0.5, 0.5, 2.0)

    def is_open(q):
        move = VELOCITY[q]
        return load_flag(move[2], move[0], move[1]) > limit

    return is_open


def link_flux(post, links, mz, fluid):
    total = None
    for q in range(19):
        step = VELOCITY[q][2]
        if step == 0:
            continue
        term = jnp.where(links[OPPOSITE[q]], post[q], 0.0)
        if total is None:
            total = term if step > 0 else -term
        else:
            total = total + term if step > 0 else total - term
    return (total + total) - jnp.where(fluid > 0.5, mz, 0.0)


def shifted(read, g, groups, cy, low, high):
    if cy == 1 and g == 0:
        value = pltpu.roll(read(tile(g)), 1, axis=0)
        return jnp.where(lax.broadcasted_iota(jnp.int32, value.shape, 0) == 0, low(), value)
    if cy == -1 and g == groups - 1:
        value = pltpu.roll(read(tile(g)), 7, axis=0)
        return jnp.where(lax.broadcasted_iota(jnp.int32, value.shape, 0) == 7, high(), value)
    return read(pl.ds(g * 8 - cy, 8))


def side_row(halo_ref, x, q):
    k = UP_Y.index(q) if q in UP_Y else 5 + DOWN_Y.index(q)
    return halo_ref[k, pl.ds(x, 1), :]


def tile(g):
    return pl.ds(g * 8, 8)


def parity(axis):
    return lax.rem(lax.axis_index(axis), 2)


def device_at(dx, dy):
    size_x = lax.axis_size("bx")
    size_y = lax.axis_size("by")
    at_x = lax.rem(lax.axis_index("bx") + (dx + size_x), size_x)
    at_y = lax.rem(lax.axis_index("by") + (dy + size_y), size_y)
    return at_x * size_y + at_y


def first_faces(
    f_hbm, mask_hbm, cls_hbm, rates_hbm, far_ref, near_ref,
    f_buf, mask_buf, cls_buf, rates_ref, sems, rates_sem,
):
    odd = parity("by")
    width = f_hbm.shape[1]
    length = f_hbm.shape[2]
    get_rates = pltpu.make_async_copy(rates_hbm, rates_ref, rates_sem)
    get_rates.start()
    copies = []
    for side in range(2):
        src = pl.ds(side * (length - 1), 1)
        group = [
            pltpu.make_async_copy(f_hbm.at[:, :, src, :], f_buf.at[side], sems.at[side, 0]),
            pltpu.make_async_copy(mask_hbm.at[:, src, :], mask_buf.at[side], sems.at[side, 1]),
            pltpu.make_async_copy(cls_hbm.at[:, src, :], cls_buf.at[side], sems.at[side, 2]),
        ]
        for copy in group:
            copy.start()
        copies.append(group)
    get_rates.wait()
    rates = [rates_ref[k] for k in range(4)]
    leaving = []
    for side in range(2):
        for copy in copies[side]:
            copy.wait()
        f_rows = f_buf.at[side].reshape(19, width, 128)
        mask_rows = mask_buf.at[side].reshape(width, 128)
        cls_rows = cls_buf.at[side].reshape(width, 128)
        for g in range(width // 8):
            fluid = mask_rows[tile(g), :] == 1
            rate = cell_rate(cls_rows[tile(g), :], fluid, rates)
            post, _ = collide([f_rows[q, tile(g), :] for q in range(19)], rate)
            values = [post[q] for q in (UP_Y if side else DOWN_Y)]
            leaving.append(values + [jnp.where(fluid, 1.0, 0.0)])
    for g in range(width // 8):
        for k in range(6):
            low = leaving[g][k]
            high = leaving[width // 8 + g][k]
            far_ref[k, tile(g), :] = jnp.where(odd == 0, low, high)
            near_ref[k, tile(g), :] = jnp.where(odd == 0, high, low)


def first_step(
    f_hbm, mask_hbm, cls_hbm, rates_hbm, order_ref,
    post_ref, flag_ref, flag_hbm, rate_ref, edge_ref, edge_flag, edge_rate, face_ref,
    f_buf, mask_ref, cls_ref, rates_ref, sems, small_sems, flag_sems,
):
    del order_ref
    width, length = mask_ref.shape[:2]
    groups = length // 8
    chunk = width // sems.shape[0]
    ahead = 4
    small = [
        pltpu.make_async_copy(rates_hbm, rates_ref, small_sems.at[0]),
        pltpu.make_async_copy(mask_hbm, mask_ref, small_sems.at[1]),
        pltpu.make_async_copy(cls_hbm, cls_ref, small_sems.at[2]),
    ]

    def fetch(c):
        planes = pl.ds(c * chunk, chunk)
        return pltpu.make_async_copy(f_hbm.at[:, planes], f_buf.at[:, planes], sems.at[c])

    def keep(c):
        planes = pl.ds(c * chunk, chunk)
        return pltpu.make_async_copy(flag_ref.at[:, planes], flag_hbm.at[:, planes], flag_sems.at[c])

    for copy in small:
        copy.start()
    for c in range(ahead):
        fetch(c).start()
    for copy in small:
        copy.wait()
    rates = [rates_ref[k] for k in range(4)]

    def part(c, carry):
        fetch(c).wait()

        @pl.when(c + ahead < width // chunk)
        def _():
            fetch(c + ahead).start()

        def plane(x, carry):
            for g in range(groups):
                fluid = mask_ref[x, tile(g), :] == 1
                rate = cell_rate(cls_ref[x, tile(g), :], fluid, rates)
                post, _ = collide([f_buf[q, x, tile(g), :] for q in range(19)], rate)
                for q in range(19):
                    post_ref[q, x, tile(g), :] = post[q]
                rate_ref[x, tile(g), :] = rate
                flag = jnp.where(fluid, 1.0, 0.0)
                for step in (-1, 0, 1):
                    flag_ref[step + 1, x, tile(g), :] = turn(flag, step)
            return carry

        lax.fori_loop(c * chunk, (c + 1) * chunk, plane, 0)
        keep(c).start()
        return carry

    lax.fori_loop(0, width // chunk, part, 0)
    for e, x in enumerate((0, 1, width - 2, width - 1)):
        for g in range(groups):
            for q in range(19):
                edge_ref[q, e, tile(g), :] = post_ref[q, x, tile(g), :]
            for s in range(3):
                edge_flag[s, e, tile(g), :] = flag_ref[s, x, tile(g), :]
    for s, x in enumerate((0, width - 1)):
        leaving = UP_X if s else DOWN_X
        for g in range(groups):
            edge_rate[s, tile(g), :] = rate_ref[x, tile(g), :]
            for k in range(5):
                face_ref[s * 6 + k, tile(g), :] = post_ref[leaving[k], x, tile(g), :]
            face_ref[s * 6 + 5, tile(g), :] = flag_ref[1, x, tile(g), :]

    def finish(c, carry):
        keep(c).wait()
        return carry

    lax.fori_loop(0, width // chunk, finish, 0)


def join_sides(
    face_ref, far_ref, near_ref,
    far_out, near_out, halo_ref, flag_ref, halo_edge, flag_edge, flag_last,
):
    odd_x = parity("bx")
    odd_y = parity("by")
    width = far_ref.shape[1]
    length = face_ref.shape[1]
    for g in range(width // 8):
        for k in range(6):
            far = far_ref[k, tile(g), :]
            near = near_ref[k, tile(g), :]
            low = jnp.where(odd_y == 0, far, near)
            high = jnp.where(odd_y == 0, near, far)
            if k < 5:
                for out_ref in (halo_ref, halo_edge):
                    out_ref[k, tile(g), :] = low
                    out_ref[5 + k, tile(g), :] = high
                continue
            for step in (-1, 0, 1):
                for side, value in enumerate((low, high)):
                    turned = turn(value, step)
                    for out_ref in (flag_ref, flag_edge, flag_last):
                        out_ref[(step + 1) * 2 + side, tile(g), :] = turned
    def put(k, at, low, high):
        far_out[k, at, :] = jnp.where(odd_x == 0, low, high)
        near_out[k, at, :] = jnp.where(odd_x == 0, high, low)

    for k in range(6):
        for g in range(length // 8):
            put(k, pl.ds(1 + g * 8, 8), face_ref[k, tile(g), :], face_ref[6 + k, tile(g), :])
        if k == 5:
            for side in range(2):
                ends = [halo_row(flag_ref, 2 + side, x) for x in (0, width - 1)]
                put(k, pl.ds(side * (length + 1), 1), *ends)
            continue
        q = DOWN_X[k]
        if q in UP_Y:
            bottom, top = side_row(halo_ref, 0, q), side_row(halo_ref, width - 1, OPPOSITE[q])
        elif q in DOWN_Y:
            bottom, top = side_row(halo_ref, width - 1, OPPOSITE[q]), side_row(halo_ref, 0, q)
        else:
            continue
        put(k, pl.ds(0, 1), bottom, bottom)
        put(k, pl.ds(length + 1, 1), top, top)


def halo_row(ref, k, x):
    return ref[k, pl.ds(x, 1), :]


def second_inner(
    post_ref, flag_ref, rate_ref, halo_ref, halo_flag,
    next_hbm, sums_ref, side_ref, edge_ref, next_ref, sems,
):
    width, length = rate_ref.shape[:2]
    groups = length // 8

    def keep(x):
        return pltpu.make_async_copy(next_ref.at[:, x], next_hbm.at[:, x], sems.at[x])

    def plane(x, carry):
        flux, count = carry
        for g in range(groups):
            local = [post_ref[q, x, tile(g), :] for q in range(19)]
            fluid = flag_ref[1, x, tile(g), :]

            def load(q, cx, cy):
                return shifted(
                    lambda at: post_ref[q, x - cx, at, :], g, groups, cy,
                    lambda: side_row(halo_ref, x - cx, q),
                    lambda: side_row(halo_ref, x - cx, q),
                )

            def load_flag(cz, cx, cy):
                return shifted(
                    lambda at: flag_ref[cz + 1, x - cx, at, :], g, groups, cy,
                    lambda: halo_row(halo_flag, (cz + 1) * 2, x - cx),
                    lambda: halo_row(halo_flag, (cz + 1) * 2 + 1, x - cx),
                )

            f, links = pull(local, load, open_by_flag(load_flag, fluid))
            post, mz = collide(f, rate_ref[x, tile(g), :])
            for q in range(19):
                next_ref[q, x, tile(g), :] = post[q]
            flux = flux + link_flux(post, links, mz, fluid)
            count = count + fluid
        keep(x).start()
        return flux, count

    zero = jnp.zeros((8, 128), F32)
    flux, count = lax.fori_loop(1, width - 1, plane, (zero, zero))
    sums_ref[0] = flux
    sums_ref[1] = count
    pitch = next_ref.shape[2]
    flat = next_ref.reshape(19, width * pitch, 128)
    for g in range(width // 8):
        low_at = pl.ds(g * 8 * pitch, 8, stride=pitch)
        high_at = pl.ds(g * 8 * pitch + length - 1, 8, stride=pitch)
        for k in range(5):
            side_ref[k, tile(g), :] = flat[DOWN_Y[k], low_at, :]
            side_ref[5 + k, tile(g), :] = flat[UP_Y[k], high_at, :]
    for s, x in enumerate((1, width - 2)):
        for g in range(groups):
            for q in range(19):
                edge_ref[q, s, tile(g), :] = next_ref[q, x, tile(g), :]

    def finish(x, carry):
        keep(x).wait()
        return carry

    lax.fori_loop(1, width - 1, finish, 0)


def second_faces(
    post_ref, flag_ref, rate_ref, halo_ref, halo_flag, sums_ref, side_ref, far_ref, near_ref,
    side_far, side_near, end_far, end_near, ends_ref, ends_copy, open_ref, share_ref,
):
    odd_x = parity("bx")
    odd_y = parity("by")
    length = rate_ref.shape[1]
    width = side_ref.shape[1]
    groups = length // 8
    flux = sums_ref[0]
    count = sums_ref[1]
    for s, side in enumerate((1, -1)):
        plane_at = 0 if s == 0 else width - 1
        group = UP_X if side == 1 else DOWN_X
        own = 0 if s == 0 else 3

        def came(k, at):
            far = far_ref[k, at, :]
            near = near_ref[k, at, :]
            if side == 1:
                return jnp.where(odd_x == 0, far, near)
            return jnp.where(odd_x == 0, near, far)

        for g in range(groups):
            local = [post_ref[q, own, tile(g), :] for q in range(19)]
            fluid = flag_ref[1, own, tile(g), :]

            def load(q, cx, cy):
                if cx == side:
                    return came(group.index(q), pl.ds(1 + g * 8 - cy, 8))
                return shifted(
                    lambda at: post_ref[q, own - cx, at, :], g, groups, cy,
                    lambda: side_row(halo_ref, plane_at - cx, q),
                    lambda: side_row(halo_ref, plane_at - cx, q),
                )

            def load_flag(cz, cx, cy):
                if cx == side:
                    return turn(came(5, pl.ds(1 + g * 8 - cy, 8)), cz)
                return shifted(
                    lambda at: flag_ref[cz + 1, own - cx, at, :], g, groups, cy,
                    lambda: halo_row(halo_flag, (cz + 1) * 2, plane_at - cx),
                    lambda: halo_row(halo_flag, (cz + 1) * 2 + 1, plane_at - cx),
                )

            f, links = pull(local, load, open_by_flag(load_flag, fluid))
            post, mz = collide(f, rate_ref[s, tile(g), :])
            for q in range(19):
                ends_ref[q, s, tile(g), :] = post[q]
                ends_copy[q, s, tile(g), :] = post[q]
                if q:
                    open_ref[q - 1, s, tile(g), :] = jnp.where(links[q], 1.0, 0.0)
            flux = flux + link_flux(post, links, mz, fluid)
            count = count + fluid

    for k in range(5):
        for g in range(groups):
            low = ends_ref[DOWN_X[k], 0, tile(g), :]
            high = ends_ref[UP_X[k], 1, tile(g), :]
            end_far[k, tile(g), :] = jnp.where(odd_x == 0, low, high)
            end_near[k, tile(g), :] = jnp.where(odd_x == 0, high, low)
    for k in range(5):
        for g in range(width // 8):
            low = side_ref[k, tile(g), :]
            high = side_ref[5 + k, tile(g), :]
            side_far[k, tile(g), :] = jnp.where(odd_y == 0, low, high)
            side_near[k, tile(g), :] = jnp.where(odd_y == 0, high, low)
        for s, x in enumerate((0, width - 1)):
            low = ends_ref[DOWN_Y[k], s, pl.ds(0, 1), :]
            high = ends_ref[UP_Y[k], s, pl.ds(length - 1, 1), :]
            side_far[k, pl.ds(x, 1), :] = jnp.where(odd_y == 0, low, high)
            side_near[k, pl.ds(x, 1), :] = jnp.where(odd_y == 0, high, low)
    lane = lax.broadcasted_iota(jnp.int32, (1, 128), 1)
    total = jnp.sum(jnp.sum(flux, axis=0, keepdims=True), axis=1, keepdims=True)
    cells = jnp.sum(jnp.sum(count, axis=0, keepdims=True), axis=1, keepdims=True)
    row = jnp.where(lane < 64, total, cells)
    share_ref[...] = jnp.broadcast_to(row[None], share_ref.shape)
    for k, (q, dx, dy) in enumerate(CORNERS):
        y = length - 1 if dy == 1 else 0
        share_ref[device_at(dx, dy), 1, :] = ends_ref[q, 1 if dx == 1 else 0, y, :]


def last_inner(
    next_hbm, flag_hbm, ends_ref, halo_flag, far_ref, near_ref,
    out_hbm, halo_out, halo_ref, next_ref, flag_ref, out_buf, in_sems, flag_sem, sems,
):
    odd_y = parity("by")
    width, length = out_hbm.shape[1:3]
    groups = length // 8
    slots = out_buf.shape[0]
    ahead = 8

    def fetch(x):
        return pltpu.make_async_copy(next_hbm.at[:, x], next_ref.at[:, x], in_sems.at[x])

    for x in range(1, 3):
        fetch(x).start()
    get_flags = pltpu.make_async_copy(flag_hbm, flag_ref, flag_sem)
    get_flags.start()
    for x in range(3, 1 + ahead):
        fetch(x).start()
    for k in range(5):
        for g in range(width // 8):
            far = far_ref[k, tile(g), :]
            near = near_ref[k, tile(g), :]
            for out_ref in (halo_ref, halo_out):
                out_ref[k, tile(g), :] = jnp.where(odd_y == 0, far, near)
                out_ref[5 + k, tile(g), :] = jnp.where(odd_y == 0, near, far)

    def copy_out(x):
        slot = lax.rem(x, slots)
        return pltpu.make_async_copy(out_buf.at[slot], out_hbm.at[:, x], sems.at[slot])

    def one_plane(x, special):
        slot = lax.rem(x, slots)
        if special >= 0:
            fetch(x + 1).wait()

        @pl.when(x + ahead < width - 1)
        def _():
            fetch(x + ahead).start()

        @pl.when(x > slots)
        def _():
            copy_out(x - slots).wait()

        for g in range(groups):
            local = [next_ref[q, x, tile(g), :] for q in range(19)]

            def load(q, cx, cy):
                def read(at):
                    if special == cx and cx != 0:
                        return ends_ref[q, 0 if cx == 1 else 1, at, :]
                    return next_ref[q, x - cx, at, :]

                return shifted(
                    read, g, groups, cy,
                    lambda: side_row(halo_ref, x - cx, q),
                    lambda: side_row(halo_ref, x - cx, q),
                )

            def load_flag(cz, cx, cy):
                return shifted(
                    lambda at: flag_ref[cz + 1, x - cx, at, :], g, groups, cy,
                    lambda: halo_row(halo_flag, (cz + 1) * 2, x - cx),
                    lambda: halo_row(halo_flag, (cz + 1) * 2 + 1, x - cx),
                )

            f, _ = pull(local, load, open_by_flag(load_flag, flag_ref[1, x, tile(g), :]))
            for q in range(19):
                out_buf[slot, q, tile(g), :] = f[q]
        copy_out(x).start()

    def plane(x, carry):
        one_plane(x, 0)
        return carry

    get_flags.wait()
    fetch(1).wait()
    one_plane(1, 1)
    lax.fori_loop(2, width - 2, plane, 0)
    one_plane(width - 2, -1)

    def finish(x, carry):
        copy_out(x).wait()
        return carry

    lax.fori_loop(width - 1 - slots, width - 1, finish, 0)


def last_faces(
    out_in, ends_ref, edge_ref, open_ref, halo_ref, far_ref, near_ref, share_ref,
    out_hbm, mean_ref, came_ref, out_buf, sems,
):
    del out_in
    odd_x = parity("bx")
    width, length = out_hbm.shape[1:3]
    groups = length // 8
    copies = []
    for s, side in enumerate((1, -1)):
        group = UP_X if side == 1 else DOWN_X
        plane_at = 0 if s == 0 else width - 1
        for k in range(5):
            for g in range(groups):
                far = far_ref[k, tile(g), :]
                near = near_ref[k, tile(g), :]
                if side == 1:
                    came_ref[s, k, pl.ds(OFF + g * 8, 8), :] = jnp.where(odd_x == 0, far, near)
                else:
                    came_ref[s, k, pl.ds(OFF + g * 8, 8), :] = jnp.where(odd_x == 0, near, far)
        for k, (q, dx, dy) in enumerate(CORNERS):
            if dx == side:
                y = OFF - 1 if dy == 1 else OFF + length
                came_ref[s, group.index(q), y, :] = share_ref[device_at(-dx, -dy), 1, :]
        for g in range(groups):
            local = [ends_ref[q, s, tile(g), :] for q in range(19)]

            def load(q, cx, cy):
                if cx == side:
                    return came_ref[s, group.index(q), pl.ds(OFF + g * 8 - cy, 8), :]
                source = ends_ref if cx == 0 else edge_ref
                return shifted(
                    lambda at: source[q, s, at, :], g, groups, cy,
                    lambda: side_row(halo_ref, plane_at - cx, q),
                    lambda: side_row(halo_ref, plane_at - cx, q),
                )

            f, _ = pull(local, load, lambda q: open_ref[q - 1, s, tile(g), :] > 0.5)
            for q in range(19):
                out_buf[s, q, tile(g), :] = f[q]
        copies.append(pltpu.make_async_copy(out_buf.at[s], out_hbm.at[:, plane_at], sems.at[s]))
        copies[s].start()
    total = jnp.sum(share_ref[:, 0, :], axis=0, keepdims=True)
    lane = lax.broadcasted_iota(jnp.int32, (1, 128), 1)
    flux = jnp.sum(jnp.where(lane == 0, total, 0.0), axis=1, keepdims=True)
    cells = jnp.sum(jnp.where(lane == 127, total, 0.0), axis=1, keepdims=True)
    mean_ref[...] = jnp.broadcast_to(flux / cells, mean_ref.shape)
    for copy in copies:
        copy.wait()


def whole(count=1):
    return [pl.BlockSpec(memory_space=pltpu.VMEM)] * count


def anywhere(count=1):
    return [pl.BlockSpec(memory_space=pl.ANY)] * count


def vmem(*shape):
    return pltpu.VMEM(shape, F32)


def held(*arrays):
    return [pltpu.with_memory_space_constraint(a, pltpu.VMEM) for a in arrays]


def main_memory(*arrays):
    return [pltpu.with_memory_space_constraint(a, pltpu.HBM) for a in arrays]


def call(kernel, scratch_mib, **kwargs):
    return pl.pallas_call(
        kernel,
        compiler_params=pltpu.CompilerParams(vmem_limit_bytes=scratch_mib * MIB),
        name=kernel.__name__,
        **kwargs,
    )


def pairs_of(count):
    far = [(i, (i + 1) % count if i % 2 else (i - 1) % count) for i in range(count)]
    near = [(i, i ^ 1) for i in range(count)]
    return far, near


def exchange(far, near, axis):
    far_pairs, near_pairs = pairs_of(lax.axis_size(axis))
    return lax.ppermute(far, axis, far_pairs), lax.ppermute(near, axis, near_pairs)


def body(populations, fluid_mask, rate_class, class_rates):
    width, length, depth = fluid_mask.shape
    count = lax.axis_size("bx") * lax.axis_size("by")
    given = main_memory(populations, fluid_mask, rate_class, class_rates)

    far, near = call(
        first_faces,
        7,
        in_specs=anywhere(4),
        out_specs=whole(2),
        out_shape=[vmem(6, width, depth)] * 2,
        scratch_shapes=[
            pltpu.VMEM((2, 19, width, 1, depth), F32),
            pltpu.VMEM((2, width, 1, depth), jnp.int32),
            pltpu.VMEM((2, width, 1, depth), jnp.int32),
            pltpu.SMEM((4,), F32),
            pltpu.SemaphoreType.DMA((2, 3)),
            pltpu.SemaphoreType.DMA,
        ],
    )(*given)
    got_far, got_near = exchange(far, near, "by")

    post, flag, flag_last, rate, edge, edge_flag, edge_rate, face = call(
        first_step,
        13,
        in_specs=anywhere(5),
        out_specs=whole(2) + anywhere(1) + whole(5),
        out_shape=[
            vmem(19, width, length, depth),
            vmem(3, width, length, depth),
            pltpu.HBM((3, width, length, depth), F32),
            vmem(width, length, depth),
            vmem(19, 4, length, depth),
            vmem(3, 4, length, depth),
            vmem(2, length, depth),
            vmem(12, length, depth),
        ],
        scratch_shapes=[
            pltpu.VMEM((19, width, length, depth), F32),
            pltpu.VMEM((width, length, depth), jnp.int32),
            pltpu.VMEM((width, length, depth), jnp.int32),
            pltpu.SMEM((4,), F32),
            pltpu.SemaphoreType.DMA((16,)),
            pltpu.SemaphoreType.DMA((3,)),
            pltpu.SemaphoreType.DMA((16,)),
        ],
    )(*given, far)

    far, near, halo, halo_flag, halo_edge, halo_flag_edge, halo_flag_last = call(
        join_sides,
        2,
        in_specs=whole(3),
        out_specs=whole(7),
        out_shape=[vmem(6, length + 8, depth)] * 2
        + [vmem(10, width, depth), vmem(6, width, depth)] * 2
        + [vmem(6, width, depth)],
    )(*held(face, got_far, got_near))
    got_far, got_near = exchange(far, near, "bx")

    after, sums, side, after_edge = call(
        second_inner,
        12,
        in_specs=whole(5),
        out_specs=anywhere(1) + whole(3),
        out_shape=[
            pltpu.HBM(populations.shape, F32),
            vmem(2, 8, depth),
            vmem(10, width, depth),
            vmem(19, 2, length, depth),
        ],
        scratch_shapes=[
            pltpu.VMEM((19, width, length, depth), F32),
            pltpu.SemaphoreType.DMA((width,)),
        ],
    )(*held(post, flag, rate, halo, halo_flag))

    side_far, side_near, end_far, end_near, ends, ends_copy, open_links, share = call(
        second_faces,
        2,
        in_specs=whole(9),
        out_specs=whole(8),
        out_shape=[vmem(5, width, depth)] * 2
        + [vmem(5, length, depth)] * 2
        + [vmem(19, 2, length, depth)] * 2
        + [vmem(18, 2, length, depth), vmem(count, 2, depth)],
    )(*held(edge, edge_flag, edge_rate, halo_edge, halo_flag_edge, sums, side, got_far, got_near))
    side_far, side_near = exchange(side_far, side_near, "by")
    end_far, end_near = exchange(end_far, end_near, "bx")
    share = lax.all_to_all(share, ("bx", "by"), 0, 0)

    final, halo = call(
        last_inner,
        17,
        in_specs=anywhere(2) + whole(4),
        out_specs=anywhere(1) + whole(1),
        out_shape=[pltpu.HBM(populations.shape, F32), vmem(10, width, depth)],
        scratch_shapes=[
            pltpu.VMEM((10, width, depth), F32),
            pltpu.VMEM((19, width, length, depth), F32),
            pltpu.VMEM((3, width, length, depth), F32),
            pltpu.VMEM((12, 19, length, depth), F32),
            pltpu.SemaphoreType.DMA((width,)),
            pltpu.SemaphoreType.DMA,
            pltpu.SemaphoreType.DMA((12,)),
        ],
    )(*main_memory(after, flag_last), *held(ends, halo_flag_last, side_far, side_near))

    final, mean = call(
        last_faces,
        3,
        in_specs=anywhere(1) + whole(7),
        out_specs=anywhere(1) + whole(1),
        out_shape=[
            pltpu.HBM(populations.shape, F32),
            jax.ShapeDtypeStruct((1, depth), F32),
        ],
        scratch_shapes=[
            pltpu.VMEM((2, 5, length + 2 * OFF, depth), F32),
            pltpu.VMEM((2, 19, length, depth), F32),
            pltpu.SemaphoreType.DMA((2,)),
        ],
        input_output_aliases={0: 0},
    )(*main_memory(final), *held(ends_copy, after_edge, open_links, halo, end_far, end_near, share))
    return final, mean[0, :1]


def solution(mesh):
    placed = (P(None, "bx", "by", None), P("bx", "by", None), P("bx", "by", None), P())
    return jax.shard_map(
        body,
        mesh=mesh,
        in_specs=placed,
        out_specs=(P(None, "bx", "by", None), P()),
        check_vma=False,
    )
```

profile of v0, /device:TPU:1, one launch (start us, length us, event | category | flops | bytes accessed | tf_op | source)
XLA Modules:
  0.0 52.5 jit_solution(8717754594585924284)
XLA Ops:
  0.6 1.3 %first_faces.1 = (f32[6,32,128]{2,1,0:T(8,128)S(1)}, f32[6,32,128]{2,1,0:T(8,128)S(1)}) custom-call(f32[19,32,32,128]{3,2,1,0:T(8,128)} %f_hbm.3, s32[32,32,128]{2,1,0:T(8,128)} %mask_hbm.3, s32[32,32,128]{2,1,0:T(8,128)} %cls_hbm.3, f32[4]{0:T(128)} %rates_hbm.3), custom_call_target="tpu_custom_call" | custom-call | tf_op jit(solution)/shard_map/first_faces/pallas_call | solution.py:673
  1.9 1.5 %collective-permute-start.1 = (f32[6,32,128]{2,1,0:T(8,128)S(1)}, f32[6,32,128]{2,1,0:T(8,128)S(1)}, u32[]{:S(2)}, u32[]{:S(2)}) collective-permute-start(f32[6,32,128]{2,1,0:T(8,128)S(1)} %get-tuple-element.40), channel_id=1, source_target_pairs={{0,1},{1,0},{2,3},{3,2},{4,5},{5,4},{6,7},{7,6},{8,9},{9,8},{10,11... | collective-permute-start | bytes 294920 | tf_op jit(solution)/shard_map/ppermute | solution.py:665
  3.4 1.3 %collective-permute-start = (f32[6,32,128]{2,1,0:T(8,128)S(1)}, f32[6,32,128]{2,1,0:T(8,128)S(1)}, u32[]{:S(2)}, u32[]{:S(2)}) collective-permute-start(f32[6,32,128]{2,1,0:T(8,128)S(1)} %get-tuple-element.35.order_ref), channel_id=1, source_target_pairs={{0,15},{1,2},{2,1},{3,4},{4,3},{5,6},{6,5},{7,8},{8,7},{9,10},{10,... | collective-permute-start | bytes 294920 | tf_op jit(solution)/shard_map/ppermute | solution.py:665
  4.7 7.3 %first_step.1 = (f32[19,32,32,128]{3,2,1,0:T(8,128)S(1)}, f32[3,32,32,128]{3,2,1,0:T(8,128)S(1)}, f32[3,32,32,128]{3,2,1,0:T(8,128)}, f32[32,32,128]{2,1,0:T(8,1...) custom-call(f32[19,32,32,128]{3,2,1,0:T(8,128)} %f_hbm.3, ...), custom_call_target="tpu_custom_call" | custom-call | tf_op jit(solution)/shard_map/first_step/pallas_call | solution.py:690
  11.9 0.0 collective-permute-done.1.near_ref
  11.9 0.0 collective-permute-done.far_ref
  12.0 0.1 join_sides.1
  12.1 4.8 %collective-permute-start.2 = (f32[6,40,128]{2,1,0:T(8,128)S(1)}, f32[6,40,128]{2,1,0:T(8,128)S(1)}, u32[]{:S(2)}, u32[]{:S(2)}) collective-permute-start(f32[6,40,128]{2,1,0:T(8,128)S(1)} %get-tuple-element.52), channel_id=1, source_target_pairs={{0,112},{16,32},{32,16},{48,64},{64,48},{80,96},{96,80},{112,0},{1... | collective-permute-start | bytes 368648 | tf_op jit(solution)/shard_map/ppermute | solution.py:665
  16.9 0.0 collective-permute-start.3
  16.9 7.1 %second_inner.1 = (f32[19,32,32,128]{3,2,1,0:T(8,128)}, f32[2,8,128]{2,1,0:T(8,128)S(1)}, f32[10,32,128]{2,1,0:T(8,128)S(1)}, f32[19,2,32,128]{3,2,1,0:T(8,128)S(1)}) custom-call(f32[19,32,32,128]{3,2,1,0:T(8,128)S(1)} %get-tuple-element.36.post_ref, f32[3,32,32,128]{3,2,1,0:T(8,128)S(1)} %get-tuple-element.37.flag_ref, ...), custom_call_target="tpu_custom_call" | custom-call | tf_op jit(solution)/shard_map/second_inner/pallas_call | solution.py:727
  24.1 0.0 collective-permute-done.2.far_ref
  24.1 0.0 collective-permute-done.3.near_ref
  24.1 1.3 %second_faces.1 = (f32[5,32,128]{2,1,0:T(8,128)S(1)}, f32[5,32,128]{2,1,0:T(8,128)S(1)}, f32[5,32,128]{2,1,0:T(8,128)S(1)}, f32[5,32,128]{2,1,0:T(8,128)S(1)}, f...) custom-call(f32[19,4,32,128]{3,2,1,0:T(8,128)S(1)} %get-tuple-elemen, ...), custom_call_target="tpu_custom_call" | custom-call | tf_op jit(solution)/shard_map/second_faces/pallas_call | solution.py:744
  25.4 7.9 %all-to-all-start = ((f32[128,2,128]{2,1,0:T(2,128)}), f32[128,2,128]{2,1,0:T(2,128)S(1)}, u32[]{:S(2)}, u32[]{:S(2)}) async-start(f32[128,2,128]{2,1,0:T(2,128)} %get-tuple-element.65), calls=%async_computation | async-start | bytes 262144 | tf_op jit(solution)/shard_map/all_to_all | solution.py:756
  33.2 1.7 %collective-permute-start.4 = (f32[5,32,128]{2,1,0:T(8,128)S(1)}, f32[5,32,128]{2,1,0:T(8,128)S(1)}, u32[]{:S(2)}, u32[]{:S(2)}) collective-permute-start(f32[5,32,128]{2,1,0:T(8,128)S(1)} %get-tuple-element.56), channel_id=1, source_target_pairs={{0,15},{1,2},{2,1},{3,4},{4,3},{5,6},{6,5},{7,8},{8,7},{9,10},{10,... | collective-permute-start | bytes 245768 | tf_op jit(solution)/shard_map/ppermute | solution.py:665
  34.9 3.8 %collective-permute-start.5 = (f32[5,32,128]{2,1,0:T(8,128)S(1)}, f32[5,32,128]{2,1,0:T(8,128)S(1)}, u32[]{:S(2)}, u32[]{:S(2)}) collective-permute-start(f32[5,32,128]{2,1,0:T(8,128)S(1)} %get-tuple-element.57), channel_id=1, source_target_pairs={{0,1},{1,0},{2,3},{3,2},{4,5},{5,4},{6,7},{7,6},{8,9},{9,8},{10,11... | collective-permute-start | bytes 245768 | tf_op jit(solution)/shard_map/ppermute | solution.py:665
  38.7 3.3 %collective-permute-start.6 = (f32[5,32,128]{2,1,0:T(8,128)S(1)}, f32[5,32,128]{2,1,0:T(8,128)S(1)}, u32[]{:S(2)}, u32[]{:S(2)}) collective-permute-start(f32[5,32,128]{2,1,0:T(8,128)S(1)} %get-tuple-element.63), channel_id=1, source_target_pairs={{0,112},{16,32},{32,16},{48,64},{64,48},{80,96},{96,80},{112,0},{1... | collective-permute-start | bytes 245768 | tf_op jit(solution)/shard_map/ppermute | solution.py:665
  42.0 0.0 collective-permute-start.7
  42.0 0.0 collective-permute-done.4.far_ref
  42.0 0.0 collective-permute-done.5.near_ref
  42.0 8.9 %last_inner.1 = (f32[19,32,32,128]{3,2,1,0:T(8,128)}, f32[10,32,128]{2,1,0:T(8,128)S(1)}) custom-call(f32[19,32,32,128]{3,2,1,0:T(8,128)} %get-tuple-element.43.next_hbm, f32[3,32,32,128]{3,2,1,0:T(8,128)} %get-tuple-element.44.flag_hbm, f32[19,2,32,128]{3,2,1,0:T(8,128)S(1)} %get-tuple-element.54.ends_ref, f32[6,32,128]{2,1,0:T(8,128)S(1)} %get-tuple-element.55.halo_flag, ...), custom_call_target="tpu_custom_call" | custom-call | tf_op jit(solution)/shard_map/last_inner/pallas_call | solution.py:758
  50.9 0.0 collective-permute-done.6.far_ref
  51.0 0.0 collective-permute-done.7.near_ref
  51.0 0.0 all-to-all-done.share_ref
  51.0 1.5 %last_faces.1 = (f32[19,32,32,128]{3,2,1,0:T(8,128)}, f32[1,128]{1,0:T(1,128)}) custom-call(f32[19,32,32,128]{3,2,1,0:T(8,128)} %get-tuple-element.58.out_in, f32[19,2,32,128]{3,2,1,0:T(8,128)S(1)} %get-tuple-element.59.ends_ref, f32[19,2,32,128]{3,2,1,0:T(8,128)S(1)} %get-tuple-element.60.edge_ref, ...), custom_call_target="tpu_custom_call", output_to_operand_aliasing={{0}: (0, {})} | custom-call | tf_op jit(solution)/shard_map/last_faces/pallas_call | solution.py:775
Async XLA Ops:
  1.9 10.0 %collective-permute-start.1 = (f32[6,32,128]{2,1,0:T(8,128)S(1)}, f32[6,32,128]{2,1,0:T(8,128)S(1)}, u32[]{:S(2)}, u32[]{:S(2)}) collective-permute-start(f32[6,32,128]{2,1,0:T(8,128)S(1)} %get-tuple-element.40), channel_id=1, source_target_pairs={{0,1},{1,0},{2,3},{3,2},{4,5},{5,4},{6,7},{7,6},{8,9},{9,8},{10,11... | collective-permute-start | bytes 294920 | tf_op jit(solution)/shard_map/ppermute | solution.py:665
  3.4 8.6 %collective-permute-start = (f32[6,32,128]{2,1,0:T(8,128)S(1)}, f32[6,32,128]{2,1,0:T(8,128)S(1)}, u32[]{:S(2)}, u32[]{:S(2)}) collective-permute-start(f32[6,32,128]{2,1,0:T(8,128)S(1)} %get-tuple-element.35.order_ref), channel_id=1, source_target_pairs={{0,15},{1,2},{2,1},{3,4},{4,3},{5,6},{6,5},{7,8},{8,7},{9,10},{10,... | collective-permute-start | bytes 294920 | tf_op jit(solution)/shard_map/ppermute | solution.py:665
  12.1 12.0 %collective-permute-start.2 = (f32[6,40,128]{2,1,0:T(8,128)S(1)}, f32[6,40,128]{2,1,0:T(8,128)S(1)}, u32[]{:S(2)}, u32[]{:S(2)}) collective-permute-start(f32[6,40,128]{2,1,0:T(8,128)S(1)} %get-tuple-element.52), channel_id=1, source_target_pairs={{0,112},{16,32},{32,16},{48,64},{64,48},{80,96},{96,80},{112,0},{1... | collective-permute-start | bytes 368648 | tf_op jit(solution)/shard_map/ppermute | solution.py:665
  16.9 7.2 %collective-permute-start.3 = (f32[6,40,128]{2,1,0:T(8,128)S(1)}, f32[6,40,128]{2,1,0:T(8,128)S(1)}, u32[]{:S(2)}, u32[]{:S(2)}) collective-permute-start(f32[6,40,128]{2,1,0:T(8,128)S(1)} %get-tuple-element.53), channel_id=1, source_target_pairs={{0,16},{16,0},{32,48},{48,32},{64,80},{80,64},{96,112},{112,96},{1... | collective-permute-start | bytes 368648 | tf_op jit(solution)/shard_map/ppermute | solution.py:665
  25.4 25.6 %all-to-all-start = ((f32[128,2,128]{2,1,0:T(2,128)}), f32[128,2,128]{2,1,0:T(2,128)S(1)}, u32[]{:S(2)}, u32[]{:S(2)}) async-start(f32[128,2,128]{2,1,0:T(2,128)} %get-tuple-element.65), calls=%async_computation | async-start | bytes 262144 | tf_op jit(solution)/shard_map/all_to_all | solution.py:756
  33.2 8.8 %collective-permute-start.4 = (f32[5,32,128]{2,1,0:T(8,128)S(1)}, f32[5,32,128]{2,1,0:T(8,128)S(1)}, u32[]{:S(2)}, u32[]{:S(2)}) collective-permute-start(f32[5,32,128]{2,1,0:T(8,128)S(1)} %get-tuple-element.56), channel_id=1, source_target_pairs={{0,15},{1,2},{2,1},{3,4},{4,3},{5,6},{6,5},{7,8},{8,7},{9,10},{10,... | collective-permute-start | bytes 245768 | tf_op jit(solution)/shard_map/ppermute | solution.py:665
  34.9 7.1 %collective-permute-start.5 = (f32[5,32,128]{2,1,0:T(8,128)S(1)}, f32[5,32,128]{2,1,0:T(8,128)S(1)}, u32[]{:S(2)}, u32[]{:S(2)}) collective-permute-start(f32[5,32,128]{2,1,0:T(8,128)S(1)} %get-tuple-element.57), channel_id=1, source_target_pairs={{0,1},{1,0},{2,3},{3,2},{4,5},{5,4},{6,7},{7,6},{8,9},{9,8},{10,11... | collective-permute-start | bytes 245768 | tf_op jit(solution)/shard_map/ppermute | solution.py:665
  38.7 12.2 %collective-permute-start.6 = (f32[5,32,128]{2,1,0:T(8,128)S(1)}, f32[5,32,128]{2,1,0:T(8,128)S(1)}, u32[]{:S(2)}, u32[]{:S(2)}) collective-permute-start(f32[5,32,128]{2,1,0:T(8,128)S(1)} %get-tuple-element.63), channel_id=1, source_target_pairs={{0,112},{16,32},{32,16},{48,64},{64,48},{80,96},{96,80},{112,0},{1... | collective-permute-start | bytes 245768 | tf_op jit(solution)/shard_map/ppermute | solution.py:665
  42.0 9.0 %collective-permute-start.7 = (f32[5,32,128]{2,1,0:T(8,128)S(1)}, f32[5,32,128]{2,1,0:T(8,128)S(1)}, u32[]{:S(2)}, u32[]{:S(2)}) collective-permute-start(f32[5,32,128]{2,1,0:T(8,128)S(1)} %get-tuple-element.64), channel_id=1, source_target_pairs={{0,16},{16,0},{32,48},{48,32},{64,80},{80,64},{96,112},{112,96},{1... | collective-permute-start | bytes 245768 | tf_op jit(solution)/shard_map/ppermute | solution.py:665
where the time goes:
time: 52.9 us; the launch traced here: 52.5 us
  Pallas kernels  27.4 us (52%)
  starting transfers between devices  24.3 us (46%)
  between operations  0.73 us (1%)
    ppermute x4, starting transfers between devices, exchange(): lax.ppermute(far, axis, far_pairs)  11.1 us
    pallas_call x1, Pallas kernels, body(): call(last_inner, 17, in_specs=anywhere(2) + whole(4), out_specs=anywhere(...  8.92 us
    all_to_all x1, starting transfers between devices, body(): share = lax.all_to_all(share, ('bx', 'by'), 0, 0)  7.86 us
    pallas_call x1, Pallas kernels, body(): call(first_step, 13, in_specs=anywhere(5), out_specs=whole(2) + anywhere(...  7.26 us
    pallas_call x1, Pallas kernels, body(): call(second_inner, 12, in_specs=whole(5), out_specs=anywhere(1) + whole(3...  7.15 us
    ppermute x4, starting transfers between devices, exchange(): lax.ppermute(near, axis, near_pairs)  5.31 us
    pallas_call x1, Pallas kernels, body(): call(last_faces, 3, in_specs=anywhere(1) + whole(7), out_specs=anywhere(1...  1.49 us
    pallas_call x1, Pallas kernels, body(): call(first_faces, 7, in_specs=anywhere(4), out_specs=whole(2), out_shape=...  1.26 us
  transfers between devices with their start and end apart: 9, of which 0 were waited for; matrix products, arithmetic and copies ran while one was open for 0% of the time, Pallas kernels for 44%

commit v1 on v0

--- a/solution.py
+++ b/solution.py
@@ -138,14 +138,27 @@
     return (total + total) - jnp.where(fluid > 0.5, mz, 0.0)
 
 
-def shifted(read, g, groups, cy, low, high):
+def beyond(ref, k, plane, g, cy, spare):
+    length = ref.shape[2]
+    if not spare:
+        return pltpu.roll(ref[k, plane, tile(g), :], cy % 8, axis=0)
+    flat = ref.reshape(ref.shape[0], ref.shape[1] * length, ref.shape[3])
+    return flat[k, pl.ds(plane * length + (g * 8 - cy), 8), :]
+
+
+def shifted(ref, k, plane, g, cy, low=None, high=None, spare=False):
+    groups = ref.shape[2] // 8
     if cy == 1 and g == 0:
-        value = pltpu.roll(read(tile(g)), 1, axis=0)
+        value = beyond(ref, k, plane, g, cy, spare)
+        if low is None:
+            return value
         return jnp.where(lax.broadcasted_iota(jnp.int32, value.shape, 0) == 0, low(), value)
     if cy == -1 and g == groups - 1:
-        value = pltpu.roll(read(tile(g)), 7, axis=0)
+        value = beyond(ref, k, plane, g, cy, spare)
+        if high is None:
+            return value
         return jnp.where(lax.broadcasted_iota(jnp.int32, value.shape, 0) == 7, high(), value)
-    return read(pl.ds(g * 8 - cy, 8))
+    return ref[k, plane, pl.ds(g * 8 - cy, 8), :]
 
 
 def side_row(halo_ref, x, q):
@@ -213,81 +226,45 @@
 
 
 def first_step(
-    f_hbm, mask_hbm, cls_hbm, rates_hbm, order_ref,
-    post_ref, flag_ref, flag_hbm, rate_ref, edge_ref, edge_flag, edge_rate, face_ref,
-    f_buf, mask_ref, cls_ref, rates_ref, sems, small_sems, flag_sems,
+    f_ref, mask_ref, cls_ref, rates_hbm, order_ref,
+    post_ref, flag_ref, rate_ref, edge_ref, edge_flag, edge_rate, face_ref,
+    rates_ref, rates_sem,
 ):
     del order_ref
     width, length = mask_ref.shape[:2]
     groups = length // 8
-    chunk = width // sems.shape[0]
-    ahead = 4
-    small = [
-        pltpu.make_async_copy(rates_hbm, rates_ref, small_sems.at[0]),
-        pltpu.make_async_copy(mask_hbm, mask_ref, small_sems.at[1]),
-        pltpu.make_async_copy(cls_hbm, cls_ref, small_sems.at[2]),
-    ]
-
-    def fetch(c):
-        planes = pl.ds(c * chunk, chunk)
-        return pltpu.make_async_copy(f_hbm.at[:, planes], f_buf.at[:, planes], sems.at[c])
-
-    def keep(c):
-        planes = pl.ds(c * chunk, chunk)
-        return pltpu.make_async_copy(flag_ref.at[:, planes], flag_hbm.at[:, planes], flag_sems.at[c])
-
-    for copy in small:
-        copy.start()
-    for c in range(ahead):
-        fetch(c).start()
-    for copy in small:
-        copy.wait()
+    get_rates = pltpu.make_async_copy(rates_hbm, rates_ref, rates_sem)
+    get_rates.start()
+    get_rates.wait()
     rates = [rates_ref[k] for k in range(4)]
 
-    def part(c, carry):
-        fetch(c).wait()
-
-        @pl.when(c + ahead < width // chunk)
-        def _():
-            fetch(c + ahead).start()
-
-        def plane(x, carry):
-            for g in range(groups):
-                fluid = mask_ref[x, tile(g), :] == 1
-                rate = cell_rate(cls_ref[x, tile(g), :], fluid, rates)
-                post, _ = collide([f_buf[q, x, tile(g), :] for q in range(19)], rate)
-                for q in range(19):
-                    post_ref[q, x, tile(g), :] = post[q]
-                rate_ref[x, tile(g), :] = rate
-                flag = jnp.where(fluid, 1.0, 0.0)
-                for step in (-1, 0, 1):
-                    flag_ref[step + 1, x, tile(g), :] = turn(flag, step)
-            return carry
-
-        lax.fori_loop(c * chunk, (c + 1) * chunk, plane, 0)
-        keep(c).start()
+    def plane(x, carry):
+        for g in range(groups):
+            fluid = mask_ref[x, tile(g), :] == 1
+            rate = cell_rate(cls_ref[x, tile(g), :], fluid, rates)
+            post, _ = collide([f_ref[q, x, tile(g), :] for q in range(19)], rate)
+            for q in range(19):
+                post_ref[q, x + 1, tile(g), :] = post[q]
+            rate_ref[x, tile(g), :] = rate
+            flag = jnp.where(fluid, 1.0, 0.0)
+            for step in (-1, 0, 1):
+                flag_ref[step + 1, x + 1, tile(g), :] = turn(flag, step)
         return carry
 
-    lax.fori_loop(0, width // chunk, part, 0)
+    lax.fori_loop(0, width, plane, 0)
     for e, x in enumerate((0, 1, width - 2, width - 1)):
         for g in range(groups):
             for q in range(19):
-                edge_ref[q, e, tile(g), :] = post_ref[q, x, tile(g), :]
+                edge_ref[q, e, tile(g), :] = post_ref[q, x + 1, tile(g), :]
             for s in range(3):
-                edge_flag[s, e, tile(g), :] = flag_ref[s, x, tile(g), :]
+                edge_flag[s, e, tile(g), :] = flag_ref[s, x + 1, tile(g), :]
     for s, x in enumerate((0, width - 1)):
         leaving = UP_X if s else DOWN_X
         for g in range(groups):
             edge_rate[s, tile(g), :] = rate_ref[x, tile(g), :]
             for k in range(5):
-                face_ref[s * 6 + k, tile(g), :] = post_ref[leaving[k], x, tile(g), :]
-            face_ref[s * 6 + 5, tile(g), :] = flag_ref[1, x, tile(g), :]
-
-    def finish(c, carry):
-        keep(c).wait()
-        return carry
-
-    lax.fori_loop(0, width // chunk, finish, 0)
+                face_ref[s * 6 + k, tile(g), :] = post_ref[leaving[k], x + 1, tile(g), :]
+            face_ref[s * 6 + 5, tile(g), :] = flag_ref[1, x + 1, tile(g), :]
 
 
 def join_sides(
@@ -343,70 +320,122 @@
 
 def second_inner(
     post_ref, flag_ref, rate_ref, halo_ref, halo_flag,
-    next_hbm, sums_ref, side_ref, edge_ref, next_ref, sems,
+    out_hbm, sums_ref, side_ref, side_copy, own_flag, edge_ref, edge_flag,
+    next_ref, out_buf, sems,
 ):
     width, length = rate_ref.shape[:2]
     groups = length // 8
-
-    def keep(x):
-        return pltpu.make_async_copy(next_ref.at[:, x], next_hbm.at[:, x], sems.at[x])
-
-    def plane(x, carry):
+    chunk = out_buf.shape[2]
+    slots = out_buf.shape[0]
+
+    def collide_tile(x, g, carry):
         flux, count = carry
+        local = [post_ref[q, x + 1, tile(g), :] for q in range(19)]
+        fluid = flag_ref[1, x + 1, tile(g), :]
+
+        def load(q, cx, cy):
+            def side():
+                return side_row(halo_ref, x - cx, q)
+
+            return shifted(post_ref, q, x + 1 - cx, g, cy, side, side, spare=True)
+
+        def load_flag(cz, cx, cy):
+            return shifted(
+                flag_ref, cz + 1, x + 1 - cx, g, cy,
+                lambda: halo_row(halo_flag, (cz + 1) * 2, x - cx),
+                lambda: halo_row(halo_flag, (cz + 1) * 2 + 1, x - cx),
+                spare=True,
+            )
+
+        f, links = pull(local, load, open_by_flag(load_flag, fluid))
+        post, mz = collide(f, rate_ref[x, tile(g), :])
+        for q in range(19):
+            next_ref[q, x, tile(g), :] = post[q]
+        flux = flux + link_flux(post, links, mz, fluid)
+        count = count + fluid
+        return flux, count
+
+    def stream_tile(x, g, slot, j):
+        local = [next_ref[q, x, tile(g), :] for q in range(19)]
+
+        def load(q, cx, cy):
+            return shifted(next_ref, q, x - cx, g, cy, spare=True)
+
+        def load_flag(cz, cx, cy):
+            return shifted(flag_ref, cz + 1, x + 1 - cx, g, cy, spare=True)
+
+        f, _ = pull(local, load, open_by_flag(load_flag, flag_ref[1, x + 1, tile(g), :]))
+        for q in range(19):
+            out_buf[slot, q, j, tile(g), :] = f[q]
+
+    def copy_out(c):
+        slot = lax.rem(c, slots)
+        return pltpu.make_async_copy(
+            out_buf.at[slot], out_hbm.at[:, pl.ds(2 + c * chunk, chunk)], sems.at[slot]
+        )
+
+    def first(x, carry):
         for g in range(groups):
-            local = [post_ref[q, x, tile(g), :] for q in range(19)]
-            fluid = flag_ref[1, x, tile(g), :]
-
-            def load(q, cx, cy):
-                return shifted(
-                    lambda at: post_ref[q, x - cx, at, :], g, groups, cy,
-                    lambda: side_row(halo_ref, x - cx, q),
-                    lambda: side_row(halo_ref, x - cx, q),
-                )
-
-            def load_flag(cz, cx, cy):
-                return shifted(
-                    lambda at: flag_ref[cz + 1, x - cx, at, :], g, groups, cy,
-                    lambda: halo_row(halo_flag, (cz + 1) * 2, x - cx),
-                    lambda: halo_row(halo_flag, (cz + 1) * 2 + 1, x - cx),
-                )
-
-            f, links = pull(local, load, open_by_flag(load_flag, fluid))
-            post, mz = collide(f, rate_ref[x, tile(g), :])
-            for q in range(19):
-                next_ref[q, x, tile(g), :] = post[q]
-            flux = flux + link_flux(post, links, mz, fluid)
-            count = count + fluid
-        keep(x).start()
-        return flux, count
+            carry = collide_tile(x, g, carry)
+        return carry
 
     zero = jnp.zeros((8, 128), F32)
-    flux, count = lax.fori_loop(1, width - 1, plane, (zero, zero))
+    carry = lax.fori_loop(1, 4, first, (zero, zero))
+    parts = (width - 4) // chunk
+
+    def part(c, carry, steps=chunk):
+        slot = lax.rem(c, slots)
+
+        @pl.when(c >= slots)
+        def _():
+            copy_out(c - slots).wait()
+
+        def step(j, carry):
+            x = 2 + c * chunk + j
+            for g in range(groups):
+                carry = collide_tile(x + 2, g, carry)
+                stream_tile(x, g, slot, j)
+            return carry
+
+        carry = lax.fori_loop(0, steps, step, carry)
+        for j in range(steps, chunk):
+            for g in range(groups):
+                stream_tile(2 + c * chunk + j, g, slot, j)
+        copy_out(c).start()
+        return carry
+
+    carry = lax.fori_loop(0, parts - 1, part, carry)
+    flux, count = part(parts - 1, carry, chunk - 1)
     sums_ref[0] = flux
     sums_ref[1] = count
-    pitch = next_ref.shape[2]
-    flat = next_ref.reshape(19, width * pitch, 128)
+    flat = next_ref.reshape(19, width * length, 128)
+    flags = flag_ref.reshape(3, (width + 2) * length, 128)
     for g in range(width // 8):
-        low_at = pl.ds(g * 8 * pitch, 8, stride=pitch)
-        high_at = pl.ds(g * 8 * pitch + length - 1, 8, stride=pitch)
+        low_at = pl.ds(g * 8 * length, 8, stride=length)
+        high_at = pl.ds(g * 8 * length + length - 1, 8, stride=length)
         for k in range(5):
-            side_ref[k, tile(g), :] = flat[DOWN_Y[k], low_at, :]
-            side_ref[5 + k, tile(g), :] = flat[UP_Y[k], high_at, :]
-    for s, x in enumerate((1, width - 2)):
+            low = flat[DOWN_Y[k], low_at, :]
+            high = flat[UP_Y[k], high_at, :]
+            for to_ref in (side_ref, side_copy):
+                to_ref[k, tile(g), :] = low
+                to_ref[5 + k, tile(g), :] = high
+        own_flag[0, tile(g), :] = flags[1, pl.ds((g * 8 + 1) * length, 8, stride=length), :]
+        own_flag[1, tile(g), :] = flags[1, pl.ds((g * 8 + 2) * length - 1, 8, stride=length), :]
+    for e, x in enumerate((1, 2, width - 3, width - 2)):
         for g in range(groups):
             for q in range(19):
-                edge_ref[q, s, tile(g), :] = next_ref[q, x, tile(g), :]
-
-    def finish(x, carry):
-        keep(x).wait()
-        return carry
-
-    lax.fori_loop(1, width - 1, finish, 0)
+                edge_ref[q, e, tile(g), :] = next_ref[q, x, tile(g), :]
+    for e, x in enumerate((0, 1, 2, width - 3, width - 2, width - 1)):
+        for g in range(groups):
+            for s in range(3):
+                edge_flag[s, e, tile(g), :] = flag_ref[s, x + 1, tile(g), :]
+    for c in range(parts - slots, parts):
+        copy_out(c).wait()
 
 
 def second_faces(
     post_ref, flag_ref, rate_ref, halo_ref, halo_flag, sums_ref, side_ref, far_ref, near_ref,
-    side_far, side_near, end_far, end_near, ends_ref, ends_copy, open_ref, share_ref,
+    side_far, side_near, end_far, end_near, ends_ref, came_flag, share_ref,
 ):
     odd_x = parity("bx")
     odd_y = parity("by")
@@ -427,24 +456,27 @@
                 return jnp.where(odd_x == 0, far, near)
             return jnp.where(odd_x == 0, near, far)
 
+        for g in range(length // 8 + 1):
+            value = came(5, tile(g))
+            for step in (-1, 0, 1):
+                came_flag[step + 1, s, tile(g), :] = turn(value, step)
         for g in range(groups):
             local = [post_ref[q, own, tile(g), :] for q in range(19)]
             fluid = flag_ref[1, own, tile(g), :]
 
             def load(q, cx, cy):
+                def beside():
+                    return side_row(halo_ref, plane_at - cx, q)
+
                 if cx == side:
                     return came(group.index(q), pl.ds(1 + g * 8 - cy, 8))
-                return shifted(
-                    lambda at: post_ref[q, own - cx, at, :], g, groups, cy,
-                    lambda: side_row(halo_ref, plane_at - cx, q),
-                    lambda: side_row(halo_ref, plane_at - cx, q),
-                )
+                return shifted(post_ref, q, own - cx, g, cy, beside, beside)
 
             def load_flag(cz, cx, cy):
                 if cx == side:
-                    return turn(came(5, pl.ds(1 + g * 8 - cy, 8)), cz)
+                    return came_flag[cz + 1, s, pl.ds(1 + g * 8 - cy, 8), :]
                 return shifted(
-                    lambda at: flag_ref[cz + 1, own - cx, at, :], g, groups, cy,
+                    flag_ref, cz + 1, own - cx, g, cy,
                     lambda: halo_row(halo_flag, (cz + 1) * 2, plane_at - cx),
                     lambda: halo_row(halo_flag, (cz + 1) * 2 + 1, plane_at - cx),
                 )
@@ -453,9 +485,6 @@
             post, mz = collide(f, rate_ref[s, tile(g), :])
             for q in range(19):
                 ends_ref[q, s, tile(g), :] = post[q]
-                ends_copy[q, s, tile(g), :] = post[q]
-                if q:
-                    open_ref[q - 1, s, tile(g), :] = jnp.where(links[q], 1.0, 0.0)
             flux = flux + link_flux(post, links, mz, fluid)
             count = count + fluid
 
@@ -486,106 +515,45 @@
         share_ref[device_at(dx, dy), 1, :] = ends_ref[q, 1 if dx == 1 else 0, y, :]
 
 
-def last_inner(
-    next_hbm, flag_hbm, ends_ref, halo_flag, far_ref, near_ref,
-    out_hbm, halo_out, halo_ref, next_ref, flag_ref, out_buf, in_sems, flag_sem, sems,
+def last_faces(
+    out_in, ends_ref, edge_ref, edge_flag, came_flag, halo_flag, side_ref, own_flag,
+    side_far, side_near, far_ref, near_ref, share_ref,
+    out_hbm, mean_ref, halo_ref, came_ref, out_buf, row_buf, sems, row_sems,
 ):
+    del out_in
+    odd_x = parity("bx")
     odd_y = parity("by")
     width, length = out_hbm.shape[1:3]
     groups = length // 8
-    slots = out_buf.shape[0]
-    ahead = 8
-
-    def fetch(x):
-        return pltpu.make_async_copy(next_hbm.at[:, x], next_ref.at[:, x], in_sems.at[x])
-
-    for x in range(1, 3):
-        fetch(x).start()
-    get_flags = pltpu.make_async_copy(flag_hbm, flag_ref, flag_sem)
-    get_flags.start()
-    for x in range(3, 1 + ahead):
-        fetch(x).start()
+    copies = []
     for k in range(5):
         for g in range(width // 8):
-            far = far_ref[k, tile(g), :]
-            near = near_ref[k, tile(g), :]
-            for out_ref in (halo_ref, halo_out):
-                out_ref[k, tile(g), :] = jnp.where(odd_y == 0, far, near)
-                out_ref[5 + k, tile(g), :] = jnp.where(odd_y == 0, near, far)
-
-    def copy_out(x):
-        slot = lax.rem(x, slots)
-        return pltpu.make_async_copy(out_buf.at[slot], out_hbm.at[:, x], sems.at[slot])
-
-    def one_plane(x, special):
-        slot = lax.rem(x, slots)
-        if special >= 0:
-            fetch(x + 1).wait()
-
-        @pl.when(x + ahead < width - 1)
-        def _():
-            fetch(x + ahead).start()
-
-        @pl.when(x > slots)
-        def _():
-            copy_out(x - slots).wait()
-
-        for g in range(groups):
-            local = [next_ref[q, x, tile(g), :] for q in range(19)]
-
-            def load(q, cx, cy):
-                def read(at):
-                    if special == cx and cx != 0:
-                        return ends_ref[q, 0 if cx == 1 else 1, at, :]
-                    return next_ref[q, x - cx, at, :]
-
-                return shifted(
-                    read, g, groups, cy,
-                    lambda: side_row(halo_ref, x - cx, q),
-                    lambda: side_row(halo_ref, x - cx, q),
-                )
-
-            def load_flag(cz, cx, cy):
-                return shifted(
-                    lambda at: flag_ref[cz + 1, x - cx, at, :], g, groups, cy,
-                    lambda: halo_row(halo_flag, (cz + 1) * 2, x - cx),
-                    lambda: halo_row(halo_flag, (cz + 1) * 2 + 1, x - cx),
-                )
-
-            f, _ = pull(local, load, open_by_flag(load_flag, flag_ref[1, x, tile(g), :]))
-            for q in range(19):
-                out_buf[slot, q, tile(g), :] = f[q]
-        copy_out(x).start()
-
-    def plane(x, carry):
-        one_plane(x, 0)
-        return carry
-
-    get_flags.wait()
-    fetch(1).wait()
-    one_plane(1, 1)
-    lax.fori_loop(2, width - 2, plane, 0)
-    one_plane(width - 2, -1)
-
-    def finish(x, carry):
-        copy_out(x).wait()
-        return carry
-
-    lax.fori_loop(width - 1 - slots, width - 1, finish, 0)
-
-
-def last_faces(
-    out_in, ends_ref, edge_ref, open_ref, halo_ref, far_ref, near_ref, share_ref,
-    out_hbm, mean_ref, came_ref, out_buf, sems,
-):
-    del out_in
-    odd_x = parity("bx")
-    width, length = out_hbm.shape[1:3]
-    groups = length // 8
-    copies = []
+            far = side_far[k, tile(g), :]
+            near = side_near[k, tile(g), :]
+            halo_ref[k, tile(g), :] = jnp.where(odd_y == 0, far, near)
+            halo_ref[5 + k, tile(g), :] = jnp.where(odd_y == 0, near, far)
+
+    for side, group in enumerate((UP_Y, DOWN_Y)):
+        for k, q in enumerate(group):
+            cx, _, cz = VELOCITY[q]
+            for x in (1, 9, 17, width - 9):
+                fluid = own_flag[side, pl.ds(x, 8), :]
+                limit = jnp.where(fluid > 0.5, 0.5, 2.0)
+                is_open = halo_flag[(cz + 1) * 2 + side, pl.ds(x - cx, 8), :] > limit
+                source = turn(halo_ref[side * 5 + k, pl.ds(x - cx, 8), :], cz)
+                value = jnp.where(is_open, source, side_ref[side * 5 + k, pl.ds(x, 8), :])
+                row_buf[side * 5 + k, pl.ds(x, 8), 0, :] = value
+            planes = pl.ds(2, width - 4)
+            copy = pltpu.make_async_copy(
+                row_buf.at[side * 5 + k, planes],
+                out_hbm.at[q, planes, pl.ds(side * (length - 1), 1), :],
+                row_sems.at[side * 5 + k],
+            )
+            copy.start()
+            copies.append(copy)
+
     for s, side in enumerate((1, -1)):
         group = UP_X if side == 1 else DOWN_X
-        plane_at = 0 if s == 0 else width - 1
         for k in range(5):
             for g in range(groups):
                 far = far_ref[k, tile(g), :]
@@ -598,24 +566,46 @@
             if dx == side:
                 y = OFF - 1 if dy == 1 else OFF + length
                 came_ref[s, group.index(q), y, :] = share_ref[device_at(-dx, -dy), 1, :]
-        for g in range(groups):
-            local = [ends_ref[q, s, tile(g), :] for q in range(19)]
-
-            def load(q, cx, cy):
-                if cx == side:
-                    return came_ref[s, group.index(q), pl.ds(OFF + g * 8 - cy, 8), :]
-                source = ends_ref if cx == 0 else edge_ref
-                return shifted(
-                    lambda at: source[q, s, at, :], g, groups, cy,
-                    lambda: side_row(halo_ref, plane_at - cx, q),
-                    lambda: side_row(halo_ref, plane_at - cx, q),
-                )
-
-            f, _ = pull(local, load, lambda q: open_ref[q - 1, s, tile(g), :] > 0.5)
-            for q in range(19):
-                out_buf[s, q, tile(g), :] = f[q]
-        copies.append(pltpu.make_async_copy(out_buf.at[s], out_hbm.at[:, plane_at], sems.at[s]))
-        copies[s].start()
+        for outer in (0, 1):
+            plane_at = outer if s == 0 else width - 1 - outer
+            for g in range(groups):
+
+                def at(plane):
+                    if plane == 0:
+                        return ends_ref, s
+                    return edge_ref, plane - 1 if s == 0 else 4 - plane
+
+                own_ref, own = at(outer)
+                local = [own_ref[q, own, tile(g), :] for q in range(19)]
+
+                def load(q, cx, cy):
+                    def beside():
+                        return side_row(halo_ref, plane_at - cx, q)
+
+                    plane = outer - cx * side
+                    if plane < 0:
+                        return came_ref[s, group.index(q), pl.ds(OFF + g * 8 - cy, 8), :]
+                    ref, index = at(plane)
+                    return shifted(ref, q, index, g, cy, beside, beside)
+
+                def load_flag(cz, cx, cy):
+                    plane = outer - cx * side
+                    if plane < 0:
+                        return came_flag[cz + 1, s, pl.ds(1 + g * 8 - cy, 8), :]
+                    return shifted(
+                        edge_flag, cz + 1, plane if s == 0 else 5 - plane, g, cy,
+                        lambda: halo_row(halo_flag, (cz + 1) * 2, plane_at - cx),
+                        lambda: halo_row(halo_flag, (cz + 1) * 2 + 1, plane_at - cx),
+                    )
+
+                fluid = edge_flag[1, outer if s == 0 else 5 - outer, tile(g), :]
+                f, _ = pull(local, load, open_by_flag(load_flag, fluid))
+                for q in range(19):
+                    out_buf[s, q, outer if s == 0 else 1 - outer, tile(g), :] = f[q]
+        planes = pl.ds(0 if s == 0 else width - 2, 2)
+        copy = pltpu.make_async_copy(out_buf.at[s], out_hbm.at[:, planes], sems.at[s])
+        copy.start()
+        copies.append(copy)
     total = jnp.sum(share_ref[:, 0, :], axis=0, keepdims=True)
     lane = lax.broadcasted_iota(jnp.int32, (1, 128), 1)
     flux = jnp.sum(jnp.where(lane == 0, total, 0.0), axis=1, keepdims=True)
@@ -645,9 +635,10 @@
     return [pltpu.with_memory_space_constraint(a, pltpu.HBM) for a in arrays]
 
 
-def call(kernel, scratch_mib, **kwargs):
+def call(kernel, scratch_mib, kib=0, **kwargs):
     return pl.pallas_call(
         kernel,
+        cost_estimate=pl.CostEstimate(flops=0, bytes_accessed=kib * 1024, transcendentals=0),
         compiler_params=pltpu.CompilerParams(vmem_limit_bytes=scratch_mib * MIB),
         name=kernel.__name__,
         **kwargs,
@@ -673,6 +664,7 @@
     far, near = call(
         first_faces,
         7,
+        16384,
         in_specs=anywhere(4),
         out_specs=whole(2),
         out_shape=[vmem(6, width, depth)] * 2,
@@ -687,31 +679,22 @@
     )(*given)
     got_far, got_near = exchange(far, near, "by")
 
-    post, flag, flag_last, rate, edge, edge_flag, edge_rate, face = call(
+    post, flag, rate, edge, edge_flag, edge_rate, face = call(
         first_step,
-        13,
-        in_specs=anywhere(5),
-        out_specs=whole(2) + anywhere(1) + whole(5),
+        2,
+        in_specs=whole(3) + anywhere(2),
+        out_specs=whole(7),
         out_shape=[
-            vmem(19, width, length, depth),
-            vmem(3, width, length, depth),
-            pltpu.HBM((3, width, length, depth), F32),
+            vmem(19, width + 2, length, depth),
+            vmem(3, width + 2, length, depth),
             vmem(width, length, depth),
             vmem(19, 4, length, depth),
             vmem(3, 4, length, depth),
             vmem(2, length, depth),
             vmem(12, length, depth),
         ],
-        scratch_shapes=[
-            pltpu.VMEM((19, width, length, depth), F32),
-            pltpu.VMEM((width, length, depth), jnp.int32),
-            pltpu.VMEM((width, length, depth), jnp.int32),
-            pltpu.SMEM((4,), F32),
-            pltpu.SemaphoreType.DMA((16,)),
-            pltpu.SemaphoreType.DMA((3,)),
-            pltpu.SemaphoreType.DMA((16,)),
-        ],
-    )(*given, far)
+        scratch_shapes=[pltpu.SMEM((4,), F32), pltpu.SemaphoreType.DMA],
+    )(*held(populations, fluid_mask, rate_class), given[3], far)
 
     far, near, halo, halo_flag, halo_edge, halo_flag_edge, halo_flag_last = call(
         join_sides,
@@ -724,70 +707,63 @@
     )(*held(face, got_far, got_near))
     got_far, got_near = exchange(far, near, "bx")
 
-    after, sums, side, after_edge = call(
+    final, sums, side, side_copy, own_flag, after_edge, last_flag = call(
         second_inner,
-        12,
+        16,
         in_specs=whole(5),
-        out_specs=anywhere(1) + whole(3),
+        out_specs=anywhere(1) + whole(6),
         out_shape=[
             pltpu.HBM(populations.shape, F32),
             vmem(2, 8, depth),
             vmem(10, width, depth),
-            vmem(19, 2, length, depth),
+            vmem(10, width, depth),
+            vmem(2, width, depth),
+            vmem(19, 4, length, depth),
+            vmem(3, 6, length, depth),
         ],
         scratch_shapes=[
             pltpu.VMEM((19, width, length, depth), F32),
-            pltpu.SemaphoreType.DMA((width,)),
+            pltpu.VMEM((3, 19, 4, length, depth), F32),
+            pltpu.SemaphoreType.DMA((3,)),
         ],
     )(*held(post, flag, rate, halo, halo_flag))
 
-    side_far, side_near, end_far, end_near, ends, ends_copy, open_links, share = call(
+    side_far, side_near, end_far, end_near, ends, came_flag, share = call(
         second_faces,
         2,
         in_specs=whole(9),
-        out_specs=whole(8),
+        out_specs=whole(7),
         out_shape=[vmem(5, width, depth)] * 2
         + [vmem(5, length, depth)] * 2
-        + [vmem(19, 2, length, depth)] * 2
-        + [vmem(18, 2, length, depth), vmem(count, 2, depth)],
+        + [vmem(19, 2, length, depth), vmem(3, 2, length + 8, depth), vmem(count, 2, depth)],
     )(*held(edge, edge_flag, edge_rate, halo_edge, halo_flag_edge, sums, side, got_far, got_near))
     side_far, side_near = exchange(side_far, side_near, "by")
     end_far, end_near = exchange(end_far, end_near, "bx")
     share = lax.all_to_all(share, ("bx", "by"), 0, 0)
 
-    final, halo = call(
-        last_inner,
-        17,
-        in_specs=anywhere(2) + whole(4),
-        out_specs=anywhere(1) + whole(1),
-        out_shape=[pltpu.HBM(populations.shape, F32), vmem(10, width, depth)],
-        scratch_shapes=[
-            pltpu.VMEM((10, width, depth), F32),
-            pltpu.VMEM((19, width, length, depth), F32),
-            pltpu.VMEM((3, width, length, depth), F32),
-            pltpu.VMEM((12, 19, length, depth), F32),
-            pltpu.SemaphoreType.DMA((width,)),
-            pltpu.SemaphoreType.DMA,
-            pltpu.SemaphoreType.DMA((12,)),
-        ],
-    )(*main_memory(after, flag_last), *held(ends, halo_flag_last, side_far, side_near))
-
     final, mean = call(
         last_faces,
-        3,
-        in_specs=anywhere(1) + whole(7),
+        6,
+        in_specs=anywhere(1) + whole(12),
         out_specs=anywhere(1) + whole(1),
         out_shape=[
             pltpu.HBM(populations.shape, F32),
             jax.ShapeDtypeStruct((1, depth), F32),
         ],
         scratch_shapes=[
+            pltpu.VMEM((10, width, depth), F32),
             pltpu.VMEM((2, 5, length + 2 * OFF, depth), F32),
-            pltpu.VMEM((2, 19, length, depth), F32),
+            pltpu.VMEM((2, 19, 2, length, depth), F32),
+            pltpu.VMEM((10, width, 1, depth), F32),
             pltpu.SemaphoreType.DMA((2,)),
+            pltpu.SemaphoreType.DMA((10,)),
         ],
         input_output_aliases={0: 0},
-    )(*main_memory(final), *held(ends_copy, after_edge, open_links, halo, end_far, end_near, share))
+    )(
+        *main_memory(final),
+        *held(ends, after_edge, last_flag, came_flag, halo_flag_last, side_copy, own_flag),
+        *held(side_far, side_near, end_far, end_near, share),
+    )
     return final, mean[0, :1]
 
 

time: 52.9 us -> 49.2 us (0.930)
  Pallas kernels: 27.4 us -> 18.4 us
  waiting for transfers between devices: 0.02 us -> 3.76 us
  starting transfers between devices: 24.3 us -> 25.9 us
    pallas_call x6 -> x5, Pallas kernels: 27.3 us -> 18.3 us  [the longest x1 9.38 us: body(): call(second_inner, 16, in_specs=whole(5), out_specs=anywhere(1) + whole(6...]
    ppermute x4, waiting for transfers between devices: 0.01 us -> 3.58 us  [exchange(): lax.ppermute(far, axis, far_pairs)]
    ppermute x4, starting transfers between devices: 11.1 us -> 11.9 us  [exchange(): lax.ppermute(far, axis, far_pairs)]
    all_to_all x1, starting transfers between devices: 7.86 us -> 8.64 us  [body(): share = lax.all_to_all(share, ('bx', 'by'), 0, 0)]
  transfers between devices with their start and end apart: 9 -> 9, of which waited for: 0 -> 2; matrix products, arithmetic and copies ran while one was open for 0% -> 0% of each run, Pallas kernels for 44% -> 28%
where the time goes in v1:
time: 49.2 us; the launch traced here: 49 us
  starting transfers between devices  25.9 us (53%)
  Pallas kernels  18.4 us (37%)
  waiting for transfers between devices  3.76 us (8%)
  between operations  0.73 us (1%)
    ppermute x4, starting transfers between devices, exchange(): lax.ppermute(far, axis, far_pairs)  11.9 us
    pallas_call x1, Pallas kernels, body(): call(second_inner, 16, in_specs=whole(5), out_specs=anywhere(1) + whole(6...  9.38 us
    all_to_all x1, starting transfers between devices, body(): share = lax.all_to_all(share, ('bx', 'by'), 0, 0)  8.64 us
    ppermute x4, starting transfers between devices, exchange(): lax.ppermute(near, axis, near_pairs)  5.31 us
    pallas_call x1, Pallas kernels, body(): call(first_step, 2, in_specs=whole(3) + anywhere(2), out_specs=whole(7),...  4.33 us
    ppermute x4, waiting for transfers between devices, exchange(): lax.ppermute(far, axis, far_pairs)  3.58 us
    pallas_call x1, Pallas kernels, body(): call(last_faces, 6, in_specs=anywhere(1) + whole(12), out_specs=anywhere(...  1.98 us
    pallas_call x1, Pallas kernels, body(): call(first_faces, 7, 16384, in_specs=anywhere(4), out_specs=whole(2), out...  1.41 us
  transfers between devices with their start and end apart: 9, of which 2 were waited for; matrix products, arithmetic and copies ran while one was open for 0% of the time, Pallas kernels for 28%

profile of v1, /device:TPU:1, one launch (start us, length us, event | category | flops | bytes accessed | tf_op | source)
XLA Modules:
  0.0 49.0 jit_solution(12311331456759294755)
XLA Ops:
  0.6 0.0 copy-start.2
  0.6 0.0 copy-start.1
  0.6 0.0 copy-start
  0.7 1.4 %first_faces.1 = (f32[6,32,128]{2,1,0:T(8,128)S(1)}, f32[6,32,128]{2,1,0:T(8,128)S(1)}) custom-call(f32[19,32,32,128]{3,2,1,0:T(8,128)} %f_ref.1, s32[32,32,128]{2,1,0:T(8,128)} %mask_ref.1, s32[32,32,128]{2,1,0:T(8,128)} %cls_ref.1, f32[4]{0:T(128)} %rates_hbm.3), custom_call_target="tpu_custom_call" | custom-call | bytes 16777216 | tf_op jit(solution)/shard_map/first_faces/pallas_call | solution.py:664
  2.1 1.5 %collective-permute-start.1 = (f32[6,32,128]{2,1,0:T(8,128)S(1)}, f32[6,32,128]{2,1,0:T(8,128)S(1)}, u32[]{:S(2)}, u32[]{:S(2)}) collective-permute-start(f32[6,32,128]{2,1,0:T(8,128)S(1)} %get-tuple-element.39), channel_id=1, source_target_pairs={{0,1},{1,0},{2,3},{3,2},{4,5},{5,4},{6,7},{7,6},{8,9},{9,8},{10,11... | collective-permute-start | bytes 294920 | tf_op jit(solution)/shard_map/ppermute | solution.py:656
  3.6 1.3 %collective-permute-start = (f32[6,32,128]{2,1,0:T(8,128)S(1)}, f32[6,32,128]{2,1,0:T(8,128)S(1)}, u32[]{:S(2)}, u32[]{:S(2)}) collective-permute-start(f32[6,32,128]{2,1,0:T(8,128)S(1)} %get-tuple-element.34.order_ref), channel_id=1, source_target_pairs={{0,15},{1,2},{2,1},{3,4},{4,3},{5,6},{6,5},{7,8},{8,7},{9,10},{10,... | collective-permute-start | bytes 294920 | tf_op jit(solution)/shard_map/ppermute | solution.py:656
  4.8 0.0 copy-done.2
  4.9 0.0 copy-done.1
  4.9 0.2 copy-done
  5.1 4.3 %first_step.1 = (f32[19,34,32,128]{3,2,1,0:T(8,128)S(1)}, f32[3,34,32,128]{3,2,1,0:T(8,128)S(1)}, f32[32,32,128]{2,1,0:T(8,128)S(1)}, f32[19,4,32,128]{3,2,1,0:T...) custom-call(f32[19,32,32,128]{3,2,1,0:T(8,128)S(1)} %copy-done, ...), custom_call_target="tpu_custom_call" | custom-call | tf_op jit(solution)/shard_map/first_step/pallas_call | solution.py:682
  9.4 0.0 collective-permute-done.1.near_ref
  9.4 0.0 collective-permute-done.far_ref
  9.4 0.1 join_sides.1
  9.6 5.7 %collective-permute-start.2 = (f32[6,40,128]{2,1,0:T(8,128)S(1)}, f32[6,40,128]{2,1,0:T(8,128)S(1)}, u32[]{:S(2)}, u32[]{:S(2)}) collective-permute-start(f32[6,40,128]{2,1,0:T(8,128)S(1)} %get-tuple-element.50), channel_id=1, source_target_pairs={{0,112},{16,32},{32,16},{48,64},{64,48},{80,96},{96,80},{112,0},{1... | collective-permute-start | bytes 368648 | tf_op jit(solution)/shard_map/ppermute | solution.py:656
  15.2 0.0 collective-permute-start.3
  15.2 9.4 %second_inner.1 = (f32[19,32,32,128]{3,2,1,0:T(8,128)}, f32[2,8,128]{2,1,0:T(8,128)S(1)}, f32[10,32,128]{2,1,0:T(8,128)S(1)}, f32[10,32,128]{2,1,0:T(8,128)S(1)}...) custom-call(f32[19,34,32,128]{3,2,1,0:T(8,128)S(1)} %get-tuple-element.35.post_ref, ...), custom_call_target="tpu_custom_call" | custom-call | tf_op jit(solution)/shard_map/second_inner/pallas_call | solution.py:710
  24.6 0.0 collective-permute-done.2.far_ref
  24.6 0.0 collective-permute-done.3.near_ref
  24.7 1.2 %second_faces.1 = (f32[5,32,128]{2,1,0:T(8,128)S(1)}, f32[5,32,128]{2,1,0:T(8,128)S(1)}, f32[5,32,128]{2,1,0:T(8,128)S(1)}, f32[5,32,128]{2,1,0:T(8,128)S(1)}, f...) custom-call(f32[19,4,32,128]{3,2,1,0:T(8,128)S(1)} %get-tuple-element.43.post_ref, ...), custom_call_target="tpu_custom_call" | custom-call | tf_op jit(solution)/shard_map/second_faces/pallas_call | solution.py:731
  25.9 8.6 %all-to-all-start = ((f32[128,2,128]{2,1,0:T(2,128)}), f32[128,2,128]{2,1,0:T(2,128)S(1)}, u32[]{:S(2)}, u32[]{:S(2)}) async-start(f32[128,2,128]{2,1,0:T(2,128)} %get-tuple-element.63), calls=%async_computation | async-start | bytes 262144 | tf_op jit(solution)/shard_map/all_to_all | solution.py:742
  34.5 1.7 %collective-permute-start.4 = (f32[5,32,128]{2,1,0:T(8,128)S(1)}, f32[5,32,128]{2,1,0:T(8,128)S(1)}, u32[]{:S(2)}, u32[]{:S(2)}) collective-permute-start(f32[5,32,128]{2,1,0:T(8,128)S(1)} %get-tuple-element.59), channel_id=1, source_target_pairs={{0,15},{1,2},{2,1},{3,4},{4,3},{5,6},{6,5},{7,8},{8,7},{9,10},{10,... | collective-permute-start | bytes 245768 | tf_op jit(solution)/shard_map/ppermute | solution.py:656
  36.2 3.8 %collective-permute-start.5 = (f32[5,32,128]{2,1,0:T(8,128)S(1)}, f32[5,32,128]{2,1,0:T(8,128)S(1)}, u32[]{:S(2)}, u32[]{:S(2)}) collective-permute-start(f32[5,32,128]{2,1,0:T(8,128)S(1)} %get-tuple-element.60), channel_id=1, source_target_pairs={{0,1},{1,0},{2,3},{3,2},{4,5},{5,4},{6,7},{7,6},{8,9},{9,8},{10,11... | collective-permute-start | bytes 245768 | tf_op jit(solution)/shard_map/ppermute | solution.py:656
  40.0 3.3 %collective-permute-start.6 = (f32[5,32,128]{2,1,0:T(8,128)S(1)}, f32[5,32,128]{2,1,0:T(8,128)S(1)}, u32[]{:S(2)}, u32[]{:S(2)}) collective-permute-start(f32[5,32,128]{2,1,0:T(8,128)S(1)} %get-tuple-element.61), channel_id=1, source_target_pairs={{0,112},{16,32},{32,16},{48,64},{64,48},{80,96},{96,80},{112,0},{1... | collective-permute-start | bytes 245768 | tf_op jit(solution)/shard_map/ppermute | solution.py:656
  43.3 0.0 collective-permute-start.7
  43.3 0.0 collective-permute-done.4.side_far
  43.3 0.0 collective-permute-done.5.side_near
  43.3 3.6 %collective-permute-done.6.far_ref = f32[5,32,128]{2,1,0:T(8,128)S(1)} collective-permute-done((f32[5,32,128]{2,1,0:T(8,128)S(1)}, f32[5,32,128]{2,1,0:T(8,128)S(1)}, u32[]{:S(2)}, u32[]{:S(2)}) %collective-permute-start.6) | collective-permute-done | bytes 81952 | tf_op jit(solution)/shard_map/ppermute | solution.py:656
  46.9 0.2 collective-permute-done.7.near_ref
  47.0 0.0 all-to-all-done.share_ref
  47.0 2.0 %last_faces.1 = (f32[19,32,32,128]{3,2,1,0:T(8,128)}, f32[1,128]{1,0:T(1,128)}) custom-call(f32[19,32,32,128]{3,2,1,0:T(8,128)} %get-tuple-element.42.out_in, f32[19,2,32,128]{3,2,1,0:T(8,128)S(1)} %get-tuple-element.52.ends_ref, f32[19,4,32,128]{3,2,1,0:T(8,128)S(1)} %get-tuple-element.53.edge_ref, ...), custom_call_target="tpu_custom_call", output_to_operand_aliasing={{0}: (0, {})} | custom-call | tf_op jit(solution)/shard_map/last_faces/pallas_call | solution.py:744
Async XLA Ops:
  0.6 4.2 %copy-start.2 = (s32[32,32,128]{2,1,0:T(8,128)S(1)}, s32[32,32,128]{2,1,0:T(8,128)}, u32[]{:S(2)}) copy-start(s32[32,32,128]{2,1,0:T(8,128)} %cls_ref.1) | copy-start | bytes 1572868
  0.6 4.2 %copy-start.1 = (s32[32,32,128]{2,1,0:T(8,128)S(1)}, s32[32,32,128]{2,1,0:T(8,128)}, u32[]{:S(2)}) copy-start(s32[32,32,128]{2,1,0:T(8,128)} %mask_ref.1) | copy-start | bytes 1572868
  0.6 4.4 %copy-start = (f32[19,32,32,128]{3,2,1,0:T(8,128)S(1)}, f32[19,32,32,128]{3,2,1,0:T(8,128)}, u32[]{:S(2)}) copy-start(f32[19,32,32,128]{3,2,1,0:T(8,128)} %f_ref.1) | copy-start | bytes 29884420
  2.1 7.4 %collective-permute-start.1 = (f32[6,32,128]{2,1,0:T(8,128)S(1)}, f32[6,32,128]{2,1,0:T(8,128)S(1)}, u32[]{:S(2)}, u32[]{:S(2)}) collective-permute-start(f32[6,32,128]{2,1,0:T(8,128)S(1)} %get-tuple-element.39), channel_id=1, source_target_pairs={{0,1},{1,0},{2,3},{3,2},{4,5},{5,4},{6,7},{7,6},{8,9},{9,8},{10,11... | collective-permute-start | bytes 294920 | tf_op jit(solution)/shard_map/ppermute | solution.py:656
  3.6 5.9 %collective-permute-start = (f32[6,32,128]{2,1,0:T(8,128)S(1)}, f32[6,32,128]{2,1,0:T(8,128)S(1)}, u32[]{:S(2)}, u32[]{:S(2)}) collective-permute-start(f32[6,32,128]{2,1,0:T(8,128)S(1)} %get-tuple-element.34.order_ref), channel_id=1, source_target_pairs={{0,15},{1,2},{2,1},{3,4},{4,3},{5,6},{6,5},{7,8},{8,7},{9,10},{10,... | collective-permute-start | bytes 294920 | tf_op jit(solution)/shard_map/ppermute | solution.py:656
  9.6 15.1 %collective-permute-start.2 = (f32[6,40,128]{2,1,0:T(8,128)S(1)}, f32[6,40,128]{2,1,0:T(8,128)S(1)}, u32[]{:S(2)}, u32[]{:S(2)}) collective-permute-start(f32[6,40,128]{2,1,0:T(8,128)S(1)} %get-tuple-element.50), channel_id=1, source_target_pairs={{0,112},{16,32},{32,16},{48,64},{64,48},{80,96},{96,80},{112,0},{1... | collective-permute-start | bytes 368648 | tf_op jit(solution)/shard_map/ppermute | solution.py:656
  15.2 9.4 %collective-permute-start.3 = (f32[6,40,128]{2,1,0:T(8,128)S(1)}, f32[6,40,128]{2,1,0:T(8,128)S(1)}, u32[]{:S(2)}, u32[]{:S(2)}) collective-permute-start(f32[6,40,128]{2,1,0:T(8,128)S(1)} %get-tuple-element.51), channel_id=1, source_target_pairs={{0,16},{16,0},{32,48},{48,32},{64,80},{80,64},{96,112},{112,96},{1... | collective-permute-start | bytes 368648 | tf_op jit(solution)/shard_map/ppermute | solution.py:656
  25.9 21.2 %all-to-all-start = ((f32[128,2,128]{2,1,0:T(2,128)}), f32[128,2,128]{2,1,0:T(2,128)S(1)}, u32[]{:S(2)}, u32[]{:S(2)}) async-start(f32[128,2,128]{2,1,0:T(2,128)} %get-tuple-element.63), calls=%async_computation | async-start | bytes 262144 | tf_op jit(solution)/shard_map/all_to_all | solution.py:742
  34.5 8.8 %collective-permute-start.4 = (f32[5,32,128]{2,1,0:T(8,128)S(1)}, f32[5,32,128]{2,1,0:T(8,128)S(1)}, u32[]{:S(2)}, u32[]{:S(2)}) collective-permute-start(f32[5,32,128]{2,1,0:T(8,128)S(1)} %get-tuple-element.59), channel_id=1, source_target_pairs={{0,15},{1,2},{2,1},{3,4},{4,3},{5,6},{6,5},{7,8},{8,7},{9,10},{10,... | collective-permute-start | bytes 245768 | tf_op jit(solution)/shard_map/ppermute | solution.py:656
  36.2 7.1 %collective-permute-start.5 = (f32[5,32,128]{2,1,0:T(8,128)S(1)}, f32[5,32,128]{2,1,0:T(8,128)S(1)}, u32[]{:S(2)}, u32[]{:S(2)}) collective-permute-start(f32[5,32,128]{2,1,0:T(8,128)S(1)} %get-tuple-element.60), channel_id=1, source_target_pairs={{0,1},{1,0},{2,3},{3,2},{4,5},{5,4},{6,7},{7,6},{8,9},{9,8},{10,11... | collective-permute-start | bytes 245768 | tf_op jit(solution)/shard_map/ppermute | solution.py:656
  40.0 6.9 %collective-permute-start.6 = (f32[5,32,128]{2,1,0:T(8,128)S(1)}, f32[5,32,128]{2,1,0:T(8,128)S(1)}, u32[]{:S(2)}, u32[]{:S(2)}) collective-permute-start(f32[5,32,128]{2,1,0:T(8,128)S(1)} %get-tuple-element.61), channel_id=1, source_target_pairs={{0,112},{16,32},{32,16},{48,64},{64,48},{80,96},{96,80},{112,0},{1... | collective-permute-start | bytes 245768 | tf_op jit(solution)/shard_map/ppermute | solution.py:656
  43.3 3.8 %collective-permute-start.7 = (f32[5,32,128]{2,1,0:T(8,128)S(1)}, f32[5,32,128]{2,1,0:T(8,128)S(1)}, u32[]{:S(2)}, u32[]{:S(2)}) collective-permute-start(f32[5,32,128]{2,1,0:T(8,128)S(1)} %get-tuple-element.62), channel_id=1, source_target_pairs={{0,16},{16,0},{32,48},{48,32},{64,80},{80,64},{96,112},{112,96},{1... | collective-permute-start | bytes 245768 | tf_op jit(solution)/shard_map/ppermute | solution.py:656

commit v2 on v1

--- a/solution.py
+++ b/solution.py
@@ -31,14 +31,17 @@
 DOWN_X = [OPPOSITE[q] for q in UP_X]
 UP_Y = [q for q in range(19) if VELOCITY[q][1] == 1]
 DOWN_Y = [OPPOSITE[q] for q in UP_Y]
-CORNERS = [(7, 1, 1), (8, -1, -1), (9, 1, -1), (10, -1, 1)]
-
-OFF = 8
+FLAG, NEXT, SUMS, RATE, ROWS = 5, 6, 11, 15, 16
 F32 = jnp.float32
 MIB = 1024 * 1024
 
 
 def collide(f, rate):
+    rho, mx, my, mz = moments(f)
+    return relax(f, rho, mx, my, mz, rate), mz
+
+
+def moments(f):
     plus = {}
     diff = {}
     for q in range(1, 19, 2):
@@ -50,6 +53,10 @@
     mx = (diff[1] + diff[7]) + (diff[9] + diff[11]) + diff[13]
     my = (diff[3] + diff[7]) + (diff[15] - diff[9]) + diff[17]
     mz = (diff[5] + diff[11]) + (diff[15] - diff[13]) - diff[17]
+    return rho, mx, my, mz
+
+
+def relax(f, rho, mx, my, mz, rate):
     inv = 4.5 / rho
     ux = inv * mx
     uy = inv * my
@@ -71,23 +78,22 @@
     pair_base = {7: base + (tx + ty), 11: base + (tx + tz), 15: base + (ty + tz)}
     lean = {7: (gx, gy), 11: (gx, gz), 15: (gy, gz)}
     out = [None] * 19
-    out[0] = keep * f[0] + (rate * (1.0 / 3.0)) * base
+
+    def put(q, even, odd):
+        if f[q] is not None:
+            out[q] = keep * f[q] + (even + odd)
+        if f[q + 1] is not None:
+            out[q + 1] = keep * f[q + 1] + (even - odd)
+
+    if f[0] is not None:
+        out[0] = keep * f[0] + (rate * (1.0 / 3.0)) * base
     for q, t, g in ((1, tx, gx), (3, ty, gy), (5, tz, gz)):
-        even = r18 * (base + t)
-        odd = g + g
-        out[q] = keep * f[q] + (even + odd)
-        out[q + 1] = keep * f[q + 1] + (even - odd)
+        put(q, r18 * (base + t), g + g)
     for q in (7, 11, 15):
         one, two = lean[q]
-        even = r36 * (pair_base[q] + cross[q])
-        odd = one + two
-        out[q] = keep * f[q] + (even + odd)
-        out[q + 1] = keep * f[q + 1] + (even - odd)
-        even = r36 * (pair_base[q] - cross[q])
-        odd = one - two
-        out[q + 2] = keep * f[q + 2] + (even + odd)
-        out[q + 3] = keep * f[q + 3] + (even - odd)
-    return out, mz
+        put(q, r36 * (pair_base[q] + cross[q]), one + two)
+        put(q + 2, r36 * (pair_base[q] - cross[q]), one - two)
+    return out
 
 
 def turn(value, step):
@@ -107,10 +113,8 @@
     out = [local[0]]
     links = [None]
     for q in range(1, 19):
-        move = VELOCITY[q]
-        source = local[q] if move[0] == 0 and move[1] == 0 else load(q, move[0], move[1])
         links.append(is_open(q))
-        out.append(jnp.where(links[q], turn(source, move[2]), local[OPPOSITE[q]]))
+        out.append(jnp.where(links[q], load(q, *VELOCITY[q]), local[OPPOSITE[q]]))
     return out, links
 
 
@@ -146,22 +150,24 @@
     return flat[k, pl.ds(plane * length + (g * 8 - cy), 8), :]
 
 
-def shifted(ref, k, plane, g, cy, low=None, high=None, spare=False):
+def shifted(ref, k, plane, g, cy, low=None, high=None, spare=False, step=0):
     groups = ref.shape[2] // 8
     if cy == 1 and g == 0:
         value = beyond(ref, k, plane, g, cy, spare)
-        if low is None:
-            return value
-        return jnp.where(lax.broadcasted_iota(jnp.int32, value.shape, 0) == 0, low(), value)
+        if low is not None:
+            value = jnp.where(lax.broadcasted_iota(jnp.int32, value.shape, 0) == 0, low(), value)
+        return turn(value, step)
     if cy == -1 and g == groups - 1:
         value = beyond(ref, k, plane, g, cy, spare)
-        if high is None:
-            return value
-        return jnp.where(lax.broadcasted_iota(jnp.int32, value.shape, 0) == 7, high(), value)
-    return ref[k, plane, pl.ds(g * 8 - cy, 8), :]
+        if high is not None:
+            value = jnp.where(lax.broadcasted_iota(jnp.int32, value.shape, 0) == 7, high(), value)
+        return turn(value, step)
+    return turn(ref[k, plane, pl.ds(g * 8 - cy, 8), :], step)
 
 
 def side_row(halo_ref, x, q):
+    if isinstance(x, int) and x < 0:
+        x = 33
     k = UP_Y.index(q) if q in UP_Y else 5 + DOWN_Y.index(q)
     return halo_ref[k, pl.ds(x, 1), :]
 
@@ -172,14 +178,6 @@
 
 def parity(axis):
     return lax.rem(lax.axis_index(axis), 2)
-
-
-def device_at(dx, dy):
-    size_x = lax.axis_size("bx")
-    size_y = lax.axis_size("by")
-    at_x = lax.rem(lax.axis_index("bx") + (dx + size_x), size_x)
-    at_y = lax.rem(lax.axis_index("by") + (dy + size_y), size_y)
-    return at_x * size_y + at_y
 
 
 def first_faces(
@@ -227,7 +225,7 @@
 
 def first_step(
     f_ref, mask_ref, cls_ref, rates_hbm, order_ref,
-    post_ref, flag_ref, rate_ref, edge_ref, edge_flag, edge_rate, face_ref,
+    post_ref, flag_ref, rate_ref, edge_ref, edge_flag, edge_rate,
     rates_ref, rates_sem,
 ):
     del order_ref
@@ -259,22 +257,19 @@
             for s in range(3):
                 edge_flag[s, e, tile(g), :] = flag_ref[s, x + 1, tile(g), :]
     for s, x in enumerate((0, width - 1)):
-        leaving = UP_X if s else DOWN_X
         for g in range(groups):
             edge_rate[s, tile(g), :] = rate_ref[x, tile(g), :]
-            for k in range(5):
-                face_ref[s * 6 + k, tile(g), :] = post_ref[leaving[k], x + 1, tile(g), :]
-            face_ref[s * 6 + 5, tile(g), :] = flag_ref[1, x + 1, tile(g), :]
 
 
 def join_sides(
-    face_ref, far_ref, near_ref,
-    far_out, near_out, halo_ref, flag_ref, halo_edge, flag_edge, flag_last,
+    post_ref, edge_flag, rate_ref, far_ref, near_ref,
+    far_out, near_out, halo_ref, flag_ref, halo_edge, flag_edge, flag_last, row_ref,
 ):
     odd_x = parity("bx")
     odd_y = parity("by")
     width = far_ref.shape[1]
-    length = face_ref.shape[1]
+    length = rate_ref.shape[1]
+    groups = length // 8
     for g in range(width // 8):
         for k in range(6):
             far = far_ref[k, tile(g), :]
@@ -291,27 +286,56 @@
                     turned = turn(value, step)
                     for out_ref in (flag_ref, flag_edge, flag_last):
                         out_ref[(step + 1) * 2 + side, tile(g), :] = turned
-    def put(k, at, low, high):
-        far_out[k, at, :] = jnp.where(odd_x == 0, low, high)
-        near_out[k, at, :] = jnp.where(odd_x == 0, high, low)
-
-    for k in range(6):
-        for g in range(length // 8):
-            put(k, pl.ds(1 + g * 8, 8), face_ref[k, tile(g), :], face_ref[6 + k, tile(g), :])
-        if k == 5:
-            for side in range(2):
-                ends = [halo_row(flag_ref, 2 + side, x) for x in (0, width - 1)]
-                put(k, pl.ds(side * (length + 1), 1), *ends)
-            continue
-        q = DOWN_X[k]
-        if q in UP_Y:
-            bottom, top = side_row(halo_ref, 0, q), side_row(halo_ref, width - 1, OPPOSITE[q])
-        elif q in DOWN_Y:
-            bottom, top = side_row(halo_ref, width - 1, OPPOSITE[q]), side_row(halo_ref, 0, q)
-        else:
-            continue
-        put(k, pl.ds(0, 1), bottom, bottom)
-        put(k, pl.ds(length + 1, 1), top, top)
+
+    def outer_plane(s, g):
+        own = 0 if s == 0 else 3
+        plane_at = 0 if s == 0 else width - 1
+        leaving = DOWN_X if s == 0 else UP_X
+        arriving = UP_X if s == 0 else DOWN_X
+        local = [post_ref[q, own, tile(g), :] for q in range(19)]
+        rate = rate_ref[s, tile(g), :]
+        fluid = edge_flag[1, own, tile(g), :]
+
+        def load(q, cx, cy, cz):
+            def beside():
+                return side_row(halo_ref, plane_at - cx, q)
+
+            return shifted(post_ref, q, own - cx, g, cy, beside, beside, step=cz)
+
+        def load_flag(cz, cx, cy):
+            return shifted(
+                edge_flag, cz + 1, own - cx, g, cy,
+                lambda: halo_row(flag_ref, (cz + 1) * 2, plane_at - cx),
+                lambda: halo_row(flag_ref, (cz + 1) * 2 + 1, plane_at - cx),
+            )
+
+        is_open = open_by_flag(load_flag, fluid)
+        f = [local[0]]
+        for q in range(1, 19):
+            if q in arriving:
+                f.append(jnp.zeros_like(fluid))
+            else:
+                f.append(jnp.where(is_open(q), load(q, *VELOCITY[q]), local[OPPOSITE[q]]))
+        return [local[q] for q in leaving] + [fluid] + [f[q] for q in leaving] + list(moments(f)) + [rate]
+
+    for g in range(groups):
+        low = outer_plane(0, g)
+        high = outer_plane(1, g)
+        for k in range(ROWS):
+            far_out[k, tile(g), :] = jnp.where(odd_x == 0, low[k], high[k])
+            near_out[k, tile(g), :] = jnp.where(odd_x == 0, high[k], low[k])
+    for s, x in enumerate((0, width - 1)):
+        leaving = DOWN_X if s == 0 else UP_X
+        for q in leaving:
+            if VELOCITY[q][1] != 0:
+                at = 0 if VELOCITY[q][1] == 1 else 1
+                row_ref[s, pl.ds(at, 1), :] = side_row(halo_ref, x, q)
+        for side in range(2):
+            row_ref[s, pl.ds(2 + side, 1), :] = halo_row(flag_ref, 2 + side, x)
+    low = row_ref[0]
+    high = row_ref[1]
+    far_out[ROWS, pl.ds(0, 8), :] = jnp.where(odd_x == 0, low, high)
+    near_out[ROWS, pl.ds(0, 8), :] = jnp.where(odd_x == 0, high, low)
 
 
 def halo_row(ref, k, x):
@@ -333,11 +357,11 @@
         local = [post_ref[q, x + 1, tile(g), :] for q in range(19)]
         fluid = flag_ref[1, x + 1, tile(g), :]
 
-        def load(q, cx, cy):
+        def load(q, cx, cy, cz):
             def side():
                 return side_row(halo_ref, x - cx, q)
 
-            return shifted(post_ref, q, x + 1 - cx, g, cy, side, side, spare=True)
+            return shifted(post_ref, q, x + 1 - cx, g, cy, side, side, spare=True, step=cz)
 
         def load_flag(cz, cx, cy):
             return shifted(
@@ -358,8 +382,8 @@
     def stream_tile(x, g, slot, j):
         local = [next_ref[q, x, tile(g), :] for q in range(19)]
 
-        def load(q, cx, cy):
-            return shifted(next_ref, q, x - cx, g, cy, spare=True)
+        def load(q, cx, cy, cz):
+            return shifted(next_ref, q, x - cx, g, cy, spare=True, step=cz)
 
         def load_flag(cz, cx, cy):
             return shifted(flag_ref, cz + 1, x + 1 - cx, g, cy, spare=True)
@@ -435,7 +459,7 @@
 
 def second_faces(
     post_ref, flag_ref, rate_ref, halo_ref, halo_flag, sums_ref, side_ref, far_ref, near_ref,
-    side_far, side_near, end_far, end_near, ends_ref, came_flag, share_ref,
+    side_far, side_near, ends_ref, ghost_ref, came_flag, share_ref, came_ref,
 ):
     odd_x = parity("bx")
     odd_y = parity("by")
@@ -444,33 +468,39 @@
     groups = length // 8
     flux = sums_ref[0]
     count = sums_ref[1]
+    for k in range(ROWS + 1):
+        for g in range(groups if k < ROWS else 1):
+            far = far_ref[k, tile(g), :]
+            near = near_ref[k, tile(g), :]
+            came_ref[0, k, tile(g), :] = jnp.where(odd_x == 0, far, near)
+            came_ref[1, k, tile(g), :] = jnp.where(odd_x == 0, near, far)
     for s, side in enumerate((1, -1)):
         plane_at = 0 if s == 0 else width - 1
         group = UP_X if side == 1 else DOWN_X
         own = 0 if s == 0 else 3
 
-        def came(k, at):
-            far = far_ref[k, at, :]
-            near = near_ref[k, at, :]
-            if side == 1:
-                return jnp.where(odd_x == 0, far, near)
-            return jnp.where(odd_x == 0, near, far)
-
-        for g in range(length // 8 + 1):
-            value = came(5, tile(g))
-            for step in (-1, 0, 1):
-                came_flag[step + 1, s, tile(g), :] = turn(value, step)
+        for step in (-1, 0, 1):
+            for g in range(groups):
+                came_flag[step + 1, s, pl.ds(1 + g * 8, 8), :] = turn(came_ref[s, FLAG, tile(g), :], step)
+            for end in range(2):
+                row = turn(came_ref[s, ROWS, pl.ds(2 + end, 1), :], step)
+                came_flag[step + 1, s, pl.ds(end * (length + 1), 1), :] = row
         for g in range(groups):
             local = [post_ref[q, own, tile(g), :] for q in range(19)]
             fluid = flag_ref[1, own, tile(g), :]
 
-            def load(q, cx, cy):
+            def load(q, cx, cy, cz):
                 def beside():
                     return side_row(halo_ref, plane_at - cx, q)
 
                 if cx == side:
-                    return came(group.index(q), pl.ds(1 + g * 8 - cy, 8))
-                return shifted(post_ref, q, own - cx, g, cy, beside, beside)
+                    return shifted(
+                        came_ref, s, group.index(q), g, cy,
+                        lambda: came_ref[s, ROWS, pl.ds(0, 1), :],
+                        lambda: came_ref[s, ROWS, pl.ds(1, 1), :],
+                        step=cz,
+                    )
+                return shifted(post_ref, q, own - cx, g, cy, beside, beside, step=cz)
 
             def load_flag(cz, cx, cy):
                 if cx == side:
@@ -488,12 +518,39 @@
             flux = flux + link_flux(post, links, mz, fluid)
             count = count + fluid
 
-    for k in range(5):
-        for g in range(groups):
-            low = ends_ref[DOWN_X[k], 0, tile(g), :]
-            high = ends_ref[UP_X[k], 1, tile(g), :]
-            end_far[k, tile(g), :] = jnp.where(odd_x == 0, low, high)
-            end_near[k, tile(g), :] = jnp.where(odd_x == 0, high, low)
+            beyond_fluid = came_ref[s, FLAG, tile(g), :]
+            rho, mx, my, mz = [came_ref[s, SUMS + i, tile(g), :] for i in range(4)]
+
+            def own_flag(cz, cx, cy):
+                return shifted(
+                    flag_ref, cz + 1, own, g, cy,
+                    lambda: halo_row(halo_flag, (cz + 1) * 2, plane_at),
+                    lambda: halo_row(halo_flag, (cz + 1) * 2 + 1, plane_at),
+                )
+
+            is_open = open_by_flag(own_flag, beyond_fluid)
+            for k, toward in enumerate(group):
+                q = OPPOSITE[toward]
+                _, cy, cz = VELOCITY[q]
+
+                def beside():
+                    return side_row(halo_ref, plane_at, q)
+
+                source = shifted(post_ref, q, own, g, cy, beside, beside, step=cz)
+                value = jnp.where(is_open(q), source, came_ref[s, k, tile(g), :])
+                rho = rho + value
+                mx = mx - value if side == 1 else mx + value
+                if cy != 0:
+                    my = my + value if cy == 1 else my - value
+                if cz != 0:
+                    mz = mz + value if cz == 1 else mz - value
+            f = [None] * 19
+            for k, q in enumerate(group):
+                f[q] = came_ref[s, NEXT + k, tile(g), :]
+            post = relax(f, rho, mx, my, mz, came_ref[s, RATE, tile(g), :])
+            for k, q in enumerate(group):
+                ghost_ref[k, s, tile(g), :] = post[q]
+
     for k in range(5):
         for g in range(width // 8):
             low = side_ref[k, tile(g), :]
@@ -505,29 +562,46 @@
             high = ends_ref[UP_Y[k], s, pl.ds(length - 1, 1), :]
             side_far[k, pl.ds(x, 1), :] = jnp.where(odd_y == 0, low, high)
             side_near[k, pl.ds(x, 1), :] = jnp.where(odd_y == 0, high, low)
+        for s, group, x in ((0, UP_X, width + 1), (1, DOWN_X, width)):
+            if DOWN_Y[k] in group:
+                low = ghost_ref[group.index(DOWN_Y[k]), s, pl.ds(0, 1), :]
+                side_far[k, pl.ds(x, 1), :] = low
+                side_near[k, pl.ds(x, 1), :] = low
+    for k in range(5):
+        for s, group, x in ((0, UP_X, width + 1), (1, DOWN_X, width)):
+            if UP_Y[k] in group:
+                high = ghost_ref[group.index(UP_Y[k]), s, pl.ds(length - 1, 1), :]
+                out_low = side_far[k, pl.ds(x, 1), :]
+                side_far[k, pl.ds(x, 1), :] = jnp.where(odd_y == 0, out_low, high)
+                side_near[k, pl.ds(x, 1), :] = jnp.where(odd_y == 0, high, out_low)
     lane = lax.broadcasted_iota(jnp.int32, (1, 128), 1)
     total = jnp.sum(jnp.sum(flux, axis=0, keepdims=True), axis=1, keepdims=True)
     cells = jnp.sum(jnp.sum(count, axis=0, keepdims=True), axis=1, keepdims=True)
     row = jnp.where(lane < 64, total, cells)
     share_ref[...] = jnp.broadcast_to(row[None], share_ref.shape)
-    for k, (q, dx, dy) in enumerate(CORNERS):
-        y = length - 1 if dy == 1 else 0
-        share_ref[device_at(dx, dy), 1, :] = ends_ref[q, 1 if dx == 1 else 0, y, :]
+
+
+def mean_flow(share_ref, order_ref, mean_ref):
+    del order_ref
+    total = jnp.sum(share_ref[:, 0, :], axis=0, keepdims=True)
+    lane = lax.broadcasted_iota(jnp.int32, (1, 128), 1)
+    flux = jnp.sum(jnp.where(lane == 0, total, 0.0), axis=1, keepdims=True)
+    cells = jnp.sum(jnp.where(lane == 127, total, 0.0), axis=1, keepdims=True)
+    mean_ref[...] = jnp.broadcast_to(flux / cells, mean_ref.shape)
 
 
 def last_faces(
-    out_in, ends_ref, edge_ref, edge_flag, came_flag, halo_flag, side_ref, own_flag,
-    side_far, side_near, far_ref, near_ref, share_ref,
-    out_hbm, mean_ref, halo_ref, came_ref, out_buf, row_buf, sems, row_sems,
+    out_in, ends_ref, edge_ref, edge_flag, ghost_ref, came_flag, halo_flag, side_ref, own_flag,
+    side_far, side_near,
+    out_hbm, halo_ref, out_buf, row_buf, sems, row_sems,
 ):
     del out_in
-    odd_x = parity("bx")
     odd_y = parity("by")
     width, length = out_hbm.shape[1:3]
     groups = length // 8
     copies = []
     for k in range(5):
-        for g in range(width // 8):
+        for g in range(width // 8 + 1):
             far = side_far[k, tile(g), :]
             near = side_near[k, tile(g), :]
             halo_ref[k, tile(g), :] = jnp.where(odd_y == 0, far, near)
@@ -554,18 +628,6 @@
 
     for s, side in enumerate((1, -1)):
         group = UP_X if side == 1 else DOWN_X
-        for k in range(5):
-            for g in range(groups):
-                far = far_ref[k, tile(g), :]
-                near = near_ref[k, tile(g), :]
-                if side == 1:
-                    came_ref[s, k, pl.ds(OFF + g * 8, 8), :] = jnp.where(odd_x == 0, far, near)
-                else:
-                    came_ref[s, k, pl.ds(OFF + g * 8, 8), :] = jnp.where(odd_x == 0, near, far)
-        for k, (q, dx, dy) in enumerate(CORNERS):
-            if dx == side:
-                y = OFF - 1 if dy == 1 else OFF + length
-                came_ref[s, group.index(q), y, :] = share_ref[device_at(-dx, -dy), 1, :]
         for outer in (0, 1):
             plane_at = outer if s == 0 else width - 1 - outer
             for g in range(groups):
@@ -578,15 +640,15 @@
                 own_ref, own = at(outer)
                 local = [own_ref[q, own, tile(g), :] for q in range(19)]
 
-                def load(q, cx, cy):
+                def load(q, cx, cy, cz):
                     def beside():
                         return side_row(halo_ref, plane_at - cx, q)
 
                     plane = outer - cx * side
                     if plane < 0:
-                        return came_ref[s, group.index(q), pl.ds(OFF + g * 8 - cy, 8), :]
+                        return shifted(ghost_ref, group.index(q), s, g, cy, beside, beside, step=cz)
                     ref, index = at(plane)
-                    return shifted(ref, q, index, g, cy, beside, beside)
+                    return shifted(ref, q, index, g, cy, beside, beside, step=cz)
 
                 def load_flag(cz, cx, cy):
                     plane = outer - cx * side
@@ -606,11 +668,6 @@
         copy = pltpu.make_async_copy(out_buf.at[s], out_hbm.at[:, planes], sems.at[s])
         copy.start()
         copies.append(copy)
-    total = jnp.sum(share_ref[:, 0, :], axis=0, keepdims=True)
-    lane = lax.broadcasted_iota(jnp.int32, (1, 128), 1)
-    flux = jnp.sum(jnp.where(lane == 0, total, 0.0), axis=1, keepdims=True)
-    cells = jnp.sum(jnp.where(lane == 127, total, 0.0), axis=1, keepdims=True)
-    mean_ref[...] = jnp.broadcast_to(flux / cells, mean_ref.shape)
     for copy in copies:
         copy.wait()
 
@@ -679,11 +736,11 @@
     )(*given)
     got_far, got_near = exchange(far, near, "by")
 
-    post, flag, rate, edge, edge_flag, edge_rate, face = call(
+    post, flag, rate, edge, edge_flag, edge_rate = call(
         first_step,
         2,
         in_specs=whole(3) + anywhere(2),
-        out_specs=whole(7),
+        out_specs=whole(6),
         out_shape=[
             vmem(19, width + 2, length, depth),
             vmem(3, width + 2, length, depth),
@@ -691,7 +748,6 @@
             vmem(19, 4, length, depth),
             vmem(3, 4, length, depth),
             vmem(2, length, depth),
-            vmem(12, length, depth),
         ],
         scratch_shapes=[pltpu.SMEM((4,), F32), pltpu.SemaphoreType.DMA],
     )(*held(populations, fluid_mask, rate_class), given[3], far)
@@ -699,12 +755,13 @@
     far, near, halo, halo_flag, halo_edge, halo_flag_edge, halo_flag_last = call(
         join_sides,
         2,
-        in_specs=whole(3),
+        in_specs=whole(5),
         out_specs=whole(7),
-        out_shape=[vmem(6, length + 8, depth)] * 2
+        out_shape=[vmem(ROWS + 1, length, depth)] * 2
         + [vmem(10, width, depth), vmem(6, width, depth)] * 2
         + [vmem(6, width, depth)],
-    )(*held(face, got_far, got_near))
+        scratch_shapes=[pltpu.VMEM((2, 8, depth), F32)],
+    )(*held(edge, edge_flag, edge_rate, got_far, got_near))
     got_far, got_near = exchange(far, near, "bx")
 
     final, sums, side, side_copy, own_flag, after_edge, last_flag = call(
@@ -728,31 +785,31 @@
         ],
     )(*held(post, flag, rate, halo, halo_flag))
 
-    side_far, side_near, end_far, end_near, ends, came_flag, share = call(
+    side_far, side_near, ends, ghost, came_flag, share = call(
         second_faces,
-        2,
+        3,
         in_specs=whole(9),
-        out_specs=whole(7),
-        out_shape=[vmem(5, width, depth)] * 2
-        + [vmem(5, length, depth)] * 2
-        + [vmem(19, 2, length, depth), vmem(3, 2, length + 8, depth), vmem(count, 2, depth)],
+        out_specs=whole(6),
+        out_shape=[vmem(5, width + 8, depth)] * 2
+        + [
+            vmem(19, 2, length, depth),
+            vmem(5, 2, length, depth),
+            vmem(3, 2, length + 8, depth),
+            vmem(count, 2, depth),
+        ],
+        scratch_shapes=[pltpu.VMEM((2, ROWS + 1, length, depth), F32)],
     )(*held(edge, edge_flag, edge_rate, halo_edge, halo_flag_edge, sums, side, got_far, got_near))
     side_far, side_near = exchange(side_far, side_near, "by")
-    end_far, end_near = exchange(end_far, end_near, "bx")
     share = lax.all_to_all(share, ("bx", "by"), 0, 0)
 
-    final, mean = call(
+    final = call(
         last_faces,
         6,
-        in_specs=anywhere(1) + whole(12),
-        out_specs=anywhere(1) + whole(1),
-        out_shape=[
-            pltpu.HBM(populations.shape, F32),
-            jax.ShapeDtypeStruct((1, depth), F32),
-        ],
+        in_specs=anywhere(1) + whole(10),
+        out_specs=anywhere(1)[0],
+        out_shape=pltpu.HBM(populations.shape, F32),
         scratch_shapes=[
-            pltpu.VMEM((10, width, depth), F32),
-            pltpu.VMEM((2, 5, length + 2 * OFF, depth), F32),
+            pltpu.VMEM((10, width + 8, depth), F32),
             pltpu.VMEM((2, 19, 2, length, depth), F32),
             pltpu.VMEM((10, width, 1, depth), F32),
             pltpu.SemaphoreType.DMA((2,)),
@@ -761,9 +818,16 @@
         input_output_aliases={0: 0},
     )(
         *main_memory(final),
-        *held(ends, after_edge, last_flag, came_flag, halo_flag_last, side_copy, own_flag),
-        *held(side_far, side_near, end_far, end_near, share),
+        *held(ends, after_edge, last_flag, ghost, came_flag, halo_flag_last, side_copy, own_flag),
+        *held(side_far, side_near),
     )
+    mean = call(
+        mean_flow,
+        2,
+        in_specs=whole(1) + anywhere(1),
+        out_specs=whole(1)[0],
+        out_shape=jax.ShapeDtypeStruct((1, depth), F32),
+    )(*held(share), *main_memory(final))
     return final, mean[0, :1]
 
 

time: 49.2 us -> 45.5 us (0.925)
  starting transfers between devices: 25.9 us -> 22.6 us
  waiting for transfers between devices: 3.76 us -> 3.14 us
    ppermute x4 -> x3, waiting for transfers between devices: 3.58 us -> 0.01 us  [exchange(): lax.ppermute(far, axis, far_pairs)]
    ppermute x4 -> x3, starting transfers between devices: 11.9 us -> 8.66 us  [exchange(): lax.ppermute(far, axis, far_pairs)]
    all_to_all x1, waiting for transfers between devices: 0.01 us -> 2.18 us  [body(): share = lax.all_to_all(share, ('bx', 'by'), 0, 0)]
    ppermute x4 -> x3, waiting for transfers between devices: 0.18 us -> 0.95 us  [exchange(): lax.ppermute(near, axis, near_pairs)]
    pallas_call x4 -> x5, Pallas kernels: 7.64 us -> 7.84 us  [the longest x1 4.3 us: body(): call(first_step, 2, in_specs=whole(3) + anywhere(2), out_specs=whole(6),...]
    ppermute x4 -> x3, starting transfers between devices: 5.31 us -> 5.3 us  [exchange(): lax.ppermute(near, axis, near_pairs)]
  transfers between devices with their start and end apart: 9 -> 7, of which waited for: 2 -> 2; matrix products, arithmetic and copies ran while one was open for 0% -> 0% of each run, Pallas kernels for 28% -> 33%
where the time goes in v2:
time: 45.5 us; the launch traced here: 45.4 us
  starting transfers between devices  22.6 us (50%)
  Pallas kernels  18.6 us (41%)
  waiting for transfers between devices  3.14 us (7%)
  between operations  0.74 us (2%)
    pallas_call x1, Pallas kernels, body(): call(second_inner, 16, in_specs=whole(5), out_specs=anywhere(1) + whole(6...  9.4 us
    ppermute x3, starting transfers between devices, exchange(): lax.ppermute(far, axis, far_pairs)  8.66 us
    all_to_all x1, starting transfers between devices, body(): share = lax.all_to_all(share, ('bx', 'by'), 0, 0)  8.64 us
    ppermute x3, starting transfers between devices, exchange(): lax.ppermute(near, axis, near_pairs)  5.3 us
    pallas_call x1, Pallas kernels, body(): call(first_step, 2, in_specs=whole(3) + anywhere(2), out_specs=whole(6),...  4.3 us
    all_to_all x1, waiting for transfers between devices, body(): share = lax.all_to_all(share, ('bx', 'by'), 0, 0)  2.18 us
    pallas_call x1, Pallas kernels, body(): call(last_faces, 6, in_specs=anywhere(1) + whole(10), out_specs=anywhere(...  1.48 us
    pallas_call x1, Pallas kernels, body(): call(first_faces, 7, 16384, in_specs=anywhere(4), out_specs=whole(2), out...  1.41 us
  transfers between devices with their start and end apart: 7, of which 2 were waited for; matrix products, arithmetic and copies ran while one was open for 0% of the time, Pallas kernels for 33%

profile of v2, /device:TPU:1, one launch (start us, length us, event | category | flops | bytes accessed | tf_op | source)
XLA Modules:
  0.0 45.4 jit_solution(16358294572045252860)
XLA Ops:
  0.6 0.0 copy-start.2
  0.6 0.0 copy-start.1
  0.6 0.0 copy-start
  0.7 1.4 %first_faces.1 = (f32[6,32,128]{2,1,0:T(8,128)S(1)}, f32[6,32,128]{2,1,0:T(8,128)S(1)}) custom-call(f32[19,32,32,128]{3,2,1,0:T(8,128)} %f_ref.1, s32[32,32,128]{2,1,0:T(8,128)} %mask_ref.1, s32[32,32,128]{2,1,0:T(8,128)} %cls_ref.1, f32[4]{0:T(128)} %rates_hbm.3), custom_call_target="tpu_custom_call" | custom-call | bytes 16777216 | tf_op jit(solution)/shard_map/first_faces/pallas_call | solution.py:721
  2.1 1.5 %collective-permute-start.1 = (f32[6,32,128]{2,1,0:T(8,128)S(1)}, f32[6,32,128]{2,1,0:T(8,128)S(1)}, u32[]{:S(2)}, u32[]{:S(2)}) collective-permute-start(f32[6,32,128]{2,1,0:T(8,128)S(1)} %get-tuple-element.37), channel_id=1, source_target_pairs={{0,1},{1,0},{2,3},{3,2},{4,5},{5,4},{6,7},{7,6},{8,9},{9,8},{10,11... | collective-permute-start | bytes 294920 | tf_op jit(solution)/shard_map/ppermute | solution.py:713
  3.6 1.3 %collective-permute-start = (f32[6,32,128]{2,1,0:T(8,128)S(1)}, f32[6,32,128]{2,1,0:T(8,128)S(1)}, u32[]{:S(2)}, u32[]{:S(2)}) collective-permute-start(f32[6,32,128]{2,1,0:T(8,128)S(1)} %get-tuple-element.30.order_ref), channel_id=1, source_target_pairs={{0,15},{1,2},{2,1},{3,4},{4,3},{5,6},{6,5},{7,8},{8,7},{9,10},{10,... | collective-permute-start | bytes 294920 | tf_op jit(solution)/shard_map/ppermute | solution.py:713
  4.8 0.0 copy-done.2
  4.9 0.0 copy-done.1
  4.9 0.2 copy-done
  5.1 4.3 %first_step.1 = (f32[19,34,32,128]{3,2,1,0:T(8,128)S(1)}, f32[3,34,32,128]{3,2,1,0:T(8,128)S(1)}, f32[32,32,128]{2,1,0:T(8,128)S(1)}, f32[19,4,32,128]{3,2,1,0:T...) custom-call(f32[19,32,32,128]{3,2,1,0:T(8,128)S(1)} %copy-done, s32[32,32,128]{2,1,0:T(8,128)S(1)} %copy-done.1, ...), custom_call_target="tpu_custom_call" | custom-call | tf_op jit(solution)/shard_map/first_step/pallas_call | solution.py:739
  9.4 0.0 collective-permute-done.1.near_ref
  9.4 0.0 collective-permute-done.far_ref
  9.4 0.2 join_sides.1
  9.6 5.7 %collective-permute-start.2 = (f32[17,32,128]{2,1,0:T(8,128)S(1)}, f32[17,32,128]{2,1,0:T(8,128)S(1)}, u32[]{:S(2)}, u32[]{:S(2)}) collective-permute-start(f32[17,32,128]{2,1,0:T(8,128)S(1)} %get-tuple-element.45), channel_id=1, source_target_pairs={{0,112},{16,32},{32,16},{48,64},{64,48},{80,96},{96,80},{112,0},{1... | collective-permute-start | bytes 835592 | tf_op jit(solution)/shard_map/ppermute | solution.py:713
  15.3 0.0 collective-permute-start.3
  15.3 9.4 %second_inner.1 = (f32[19,32,32,128]{3,2,1,0:T(8,128)}, f32[2,8,128]{2,1,0:T(8,128)S(1)}, f32[10,32,128]{2,1,0:T(8,128)S(1)}, f32[10,32,128]{2,1,0:T(8,128)S(1)}...) custom-call(f32[19,34,32,128]{3,2,1,0:T(8,128)S(1)} %get-tuple-element.31.post_ref, ...), custom_call_target="tpu_custom_call" | custom-call | tf_op jit(solution)/shard_map/second_inner/pallas_call | solution.py:767
  24.7 0.0 collective-permute-done.2.far_ref
  24.7 0.0 collective-permute-done.3.near_ref
  24.7 1.2 %second_faces.1 = (f32[5,40,128]{2,1,0:T(8,128)S(1)}, f32[5,40,128]{2,1,0:T(8,128)S(1)}, f32[19,2,32,128]{3,2,1,0:T(8,128)S(1)}, f32[5,2,32,128]{3,2,1,0:T(8,128...) custom-call(f32[19,4,32,128]{3,2,1,0:T(8,128)S(1)} %get-tuple-element.34.post_ref, ...), custom_call_target="tpu_custom_call" | custom-call | tf_op jit(solution)/shard_map/second_faces/pallas_call | solution.py:788
  25.9 8.6 %all-to-all-start = ((f32[128,2,128]{2,1,0:T(2,128)}), f32[128,2,128]{2,1,0:T(2,128)S(1)}, u32[]{:S(2)}, u32[]{:S(2)}) async-start(f32[128,2,128]{2,1,0:T(2,128)} %get-tuple-element.57), calls=%async_computation | async-start | bytes 262144 | tf_op jit(solution)/shard_map/all_to_all | solution.py:803
  34.6 1.7 %collective-permute-start.4 = (f32[5,40,128]{2,1,0:T(8,128)S(1)}, f32[5,40,128]{2,1,0:T(8,128)S(1)}, u32[]{:S(2)}, u32[]{:S(2)}) collective-permute-start(f32[5,40,128]{2,1,0:T(8,128)S(1)} %get-tuple-element.55), channel_id=1, source_target_pairs={{0,15},{1,2},{2,1},{3,4},{4,3},{5,6},{6,5},{7,8},{8,7},{9,10},{10,... | collective-permute-start | bytes 307208 | tf_op jit(solution)/shard_map/ppermute | solution.py:713
  36.3 3.8 %collective-permute-start.5 = (f32[5,40,128]{2,1,0:T(8,128)S(1)}, f32[5,40,128]{2,1,0:T(8,128)S(1)}, u32[]{:S(2)}, u32[]{:S(2)}) collective-permute-start(f32[5,40,128]{2,1,0:T(8,128)S(1)} %get-tuple-element.56), channel_id=1, source_target_pairs={{0,1},{1,0},{2,3},{3,2},{4,5},{5,4},{6,7},{7,6},{8,9},{9,8},{10,11... | collective-permute-start | bytes 307208 | tf_op jit(solution)/shard_map/ppermute | solution.py:713
  40.1 0.0 collective-permute-done.4.side_far
  40.1 0.9 %collective-permute-done.5.side_near = f32[5,40,128]{2,1,0:T(8,128)S(1)} collective-permute-done((f32[5,40,128]{2,1,0:T(8,128)S(1)}, f32[5,40,128]{2,1,0:T(8,128)S(1)}, u32[]{:S(2)}, u32[]{:S(2)}) %collective-permute-start.5) | collective-permute-done | bytes 102432 | tf_op jit(solution)/shard_map/ppermute | solution.py:713
  41.1 1.5 %last_faces.1.order_ref = f32[19,32,32,128]{3,2,1,0:T(8,128)} custom-call(f32[19,32,32,128]{3,2,1,0:T(8,128)} %get-tuple-element.40.out_in, f32[19,2,32,128]{3,2,1,0:T(8,128)S(1)} %get-tuple-element.47.ends_ref, f32[19,4,32,128]{3,2,1,0:T(8,128)S(1)} %get-tuple-element.48.edge_ref, ...), custom_call_target="tpu_custom_call", output_to_operand_aliasing={{}: (0, {})} | custom-call | tf_op jit(solution)/shard_map/last_faces/pallas_call | solution.py:805
  42.5 2.2 %all-to-all-done.share_ref = f32[128,2,128]{2,1,0:T(2,128)S(1)} async-done(((f32[128,2,128]{2,1,0:T(2,128)}), f32[128,2,128]{2,1,0:T(2,128)S(1)}, u32[]{:S(2)}, u32[]{:S(2)}) %all-to-all-start) | async-done | bytes 131104 | tf_op jit(solution)/shard_map/all_to_all | solution.py:803
  44.7 0.6 %mean_flow.1 = f32[1,128]{1,0:T(1,128)} custom-call(f32[128,2,128]{2,1,0:T(2,128)S(1)} %all-to-all-done.share_ref, f32[19,32,32,128]{3,2,1,0:T(8,128)} %last_faces.1.order_ref), custom_call_target="tpu_custom_call" | custom-call | tf_op jit(solution)/shard_map/mean_flow/pallas_call | solution.py:824
Async XLA Ops:
  0.6 4.2 %copy-start.2 = (s32[32,32,128]{2,1,0:T(8,128)S(1)}, s32[32,32,128]{2,1,0:T(8,128)}, u32[]{:S(2)}) copy-start(s32[32,32,128]{2,1,0:T(8,128)} %cls_ref.1) | copy-start | bytes 1572868
  0.6 4.2 %copy-start.1 = (s32[32,32,128]{2,1,0:T(8,128)S(1)}, s32[32,32,128]{2,1,0:T(8,128)}, u32[]{:S(2)}) copy-start(s32[32,32,128]{2,1,0:T(8,128)} %mask_ref.1) | copy-start | bytes 1572868
  0.6 4.4 %copy-start = (f32[19,32,32,128]{3,2,1,0:T(8,128)S(1)}, f32[19,32,32,128]{3,2,1,0:T(8,128)}, u32[]{:S(2)}) copy-start(f32[19,32,32,128]{3,2,1,0:T(8,128)} %f_ref.1) | copy-start | bytes 29884420
  2.1 7.3 %collective-permute-start.1 = (f32[6,32,128]{2,1,0:T(8,128)S(1)}, f32[6,32,128]{2,1,0:T(8,128)S(1)}, u32[]{:S(2)}, u32[]{:S(2)}) collective-permute-start(f32[6,32,128]{2,1,0:T(8,128)S(1)} %get-tuple-element.37), channel_id=1, source_target_pairs={{0,1},{1,0},{2,3},{3,2},{4,5},{5,4},{6,7},{7,6},{8,9},{9,8},{10,11... | collective-permute-start | bytes 294920 | tf_op jit(solution)/shard_map/ppermute | solution.py:713
  3.6 5.8 %collective-permute-start = (f32[6,32,128]{2,1,0:T(8,128)S(1)}, f32[6,32,128]{2,1,0:T(8,128)S(1)}, u32[]{:S(2)}, u32[]{:S(2)}) collective-permute-start(f32[6,32,128]{2,1,0:T(8,128)S(1)} %get-tuple-element.30.order_ref), channel_id=1, source_target_pairs={{0,15},{1,2},{2,1},{3,4},{4,3},{5,6},{6,5},{7,8},{8,7},{9,10},{10,... | collective-permute-start | bytes 294920 | tf_op jit(solution)/shard_map/ppermute | solution.py:713
  9.6 15.1 %collective-permute-start.2 = (f32[17,32,128]{2,1,0:T(8,128)S(1)}, f32[17,32,128]{2,1,0:T(8,128)S(1)}, u32[]{:S(2)}, u32[]{:S(2)}) collective-permute-start(f32[17,32,128]{2,1,0:T(8,128)S(1)} %get-tuple-element.45), channel_id=1, source_target_pairs={{0,112},{16,32},{32,16},{48,64},{64,48},{80,96},{96,80},{112,0},{1... | collective-permute-start | bytes 835592 | tf_op jit(solution)/shard_map/ppermute | solution.py:713
  15.3 9.4 %collective-permute-start.3 = (f32[17,32,128]{2,1,0:T(8,128)S(1)}, f32[17,32,128]{2,1,0:T(8,128)S(1)}, u32[]{:S(2)}, u32[]{:S(2)}) collective-permute-start(f32[17,32,128]{2,1,0:T(8,128)S(1)} %get-tuple-element.46), channel_id=1, source_target_pairs={{0,16},{16,0},{32,48},{48,32},{64,80},{80,64},{96,112},{112,96},{1... | collective-permute-start | bytes 835592 | tf_op jit(solution)/shard_map/ppermute | solution.py:713
  25.9 18.8 %all-to-all-start = ((f32[128,2,128]{2,1,0:T(2,128)}), f32[128,2,128]{2,1,0:T(2,128)S(1)}, u32[]{:S(2)}, u32[]{:S(2)}) async-start(f32[128,2,128]{2,1,0:T(2,128)} %get-tuple-element.57), calls=%async_computation | async-start | bytes 262144 | tf_op jit(solution)/shard_map/all_to_all | solution.py:803
  34.6 5.5 %collective-permute-start.4 = (f32[5,40,128]{2,1,0:T(8,128)S(1)}, f32[5,40,128]{2,1,0:T(8,128)S(1)}, u32[]{:S(2)}, u32[]{:S(2)}) collective-permute-start(f32[5,40,128]{2,1,0:T(8,128)S(1)} %get-tuple-element.55), channel_id=1, source_target_pairs={{0,15},{1,2},{2,1},{3,4},{4,3},{5,6},{6,5},{7,8},{8,7},{9,10},{10,... | collective-permute-start | bytes 307208 | tf_op jit(solution)/shard_map/ppermute | solution.py:713
  36.3 4.7 %collective-permute-start.5 = (f32[5,40,128]{2,1,0:T(8,128)S(1)}, f32[5,40,128]{2,1,0:T(8,128)S(1)}, u32[]{:S(2)}, u32[]{:S(2)}) collective-permute-start(f32[5,40,128]{2,1,0:T(8,128)S(1)} %get-tuple-element.56), channel_id=1, source_target_pairs={{0,1},{1,0},{2,3},{3,2},{4,5},{5,4},{6,7},{7,6},{8,9},{9,8},{10,11... | collective-permute-start | bytes 307208 | tf_op jit(solution)/shard_map/ppermute | solution.py:713

commit v3 on v2

--- a/solution.py
+++ b/solution.py
@@ -181,7 +181,7 @@
 
 
 def first_faces(
-    f_hbm, mask_hbm, cls_hbm, rates_hbm, far_ref, near_ref,
+    f_hbm, mask_hbm, cls_hbm, rates_hbm, near_ref, far_ref, rates_out,
     f_buf, mask_buf, cls_buf, rates_ref, sems, rates_sem,
 ):
     odd = parity("by")
@@ -202,6 +202,8 @@
         copies.append(group)
     get_rates.wait()
     rates = [rates_ref[k] for k in range(4)]
+    for k in range(4):
+        rates_out[pl.ds(k, 1), :] = jnp.full((1, 128), rates[k], F32)
     leaving = []
     for side in range(2):
         for copy in copies[side]:
@@ -224,17 +226,12 @@
 
 
 def first_step(
-    f_ref, mask_ref, cls_ref, rates_hbm, order_ref,
+    f_ref, mask_ref, cls_ref, rates_ref,
     post_ref, flag_ref, rate_ref, edge_ref, edge_flag, edge_rate,
-    rates_ref, rates_sem,
 ):
-    del order_ref
     width, length = mask_ref.shape[:2]
     groups = length // 8
-    get_rates = pltpu.make_async_copy(rates_hbm, rates_ref, rates_sem)
-    get_rates.start()
-    get_rates.wait()
-    rates = [rates_ref[k] for k in range(4)]
+    rates = [jnp.broadcast_to(rates_ref[pl.ds(k, 1), :], (8, 128)) for k in range(4)]
 
     def plane(x, carry):
         for g in range(groups):
@@ -249,7 +246,7 @@
                 flag_ref[step + 1, x + 1, tile(g), :] = turn(flag, step)
         return carry
 
-    lax.fori_loop(0, width, plane, 0)
+    lax.fori_loop(0, width, plane, 0, unroll=2)
     for e, x in enumerate((0, 1, width - 2, width - 1)):
         for g in range(groups):
             for q in range(19):
@@ -262,7 +259,7 @@
 
 
 def join_sides(
-    post_ref, edge_flag, rate_ref, far_ref, near_ref,
+    post_ref, edge_flag, rate_ref, near_ref, far_ref,
     far_out, near_out, halo_ref, flag_ref, halo_edge, flag_edge, flag_last, row_ref,
 ):
     odd_x = parity("bx")
@@ -345,7 +342,7 @@
 def second_inner(
     post_ref, flag_ref, rate_ref, halo_ref, halo_flag,
     out_hbm, sums_ref, side_ref, side_copy, own_flag, edge_ref, edge_flag,
-    next_ref, out_buf, sems,
+    next_ref, out_buf, sems, last_sems,
 ):
     width, length = rate_ref.shape[:2]
     groups = length // 8
@@ -417,19 +414,32 @@
         def step(j, carry):
             x = 2 + c * chunk + j
             for g in range(groups):
+                stream_tile(x, g, slot, j)
+            for g in range(groups):
                 carry = collide_tile(x + 2, g, carry)
-                stream_tile(x, g, slot, j)
             return carry
 
-        carry = lax.fori_loop(0, steps, step, carry)
-        for j in range(steps, chunk):
-            for g in range(groups):
-                stream_tile(2 + c * chunk + j, g, slot, j)
-        copy_out(c).start()
+        carry = lax.fori_loop(0, steps, step, carry, unroll=steps if steps == chunk else 1)
+        if steps == chunk:
+            copy_out(c).start()
         return carry
 
     carry = lax.fori_loop(0, parts - 1, part, carry)
+    last_slot = (parts - 1) % slots
+    last_x = 2 + (parts - 1) * chunk
+
+    def copy_last(j, planes):
+        return pltpu.make_async_copy(
+            out_buf.at[last_slot, :, pl.ds(j, planes)],
+            out_hbm.at[:, pl.ds(last_x + j, planes)],
+            last_sems.at[j],
+        )
+
     flux, count = part(parts - 1, carry, chunk - 1)
+    copy_last(0, chunk - 1).start()
+    for g in range(groups):
+        stream_tile(last_x + chunk - 1, g, last_slot, chunk - 1)
+    copy_last(chunk - 1, 1).start()
     sums_ref[0] = flux
     sums_ref[1] = count
     flat = next_ref.reshape(19, width * length, 128)
@@ -453,13 +463,15 @@
         for g in range(groups):
             for s in range(3):
                 edge_flag[s, e, tile(g), :] = flag_ref[s, x + 1, tile(g), :]
-    for c in range(parts - slots, parts):
+    for c in range(parts - slots, parts - 1):
         copy_out(c).wait()
+    copy_last(0, chunk - 1).wait()
+    copy_last(chunk - 1, 1).wait()
 
 
 def second_faces(
     post_ref, flag_ref, rate_ref, halo_ref, halo_flag, sums_ref, side_ref, far_ref, near_ref,
-    side_far, side_near, ends_ref, ghost_ref, came_flag, share_ref, came_ref,
+    side_near, side_far, ends_ref, ghost_ref, came_flag, share_ref, came_ref,
 ):
     odd_x = parity("bx")
     odd_y = parity("by")
@@ -592,7 +604,7 @@
 
 def last_faces(
     out_in, ends_ref, edge_ref, edge_flag, ghost_ref, came_flag, halo_flag, side_ref, own_flag,
-    side_far, side_near,
+    side_near, side_far,
     out_hbm, halo_ref, out_buf, row_buf, sems, row_sems,
 ):
     del out_in
@@ -718,13 +730,13 @@
     count = lax.axis_size("bx") * lax.axis_size("by")
     given = main_memory(populations, fluid_mask, rate_class, class_rates)
 
-    far, near = call(
+    near, far, rates = call(
         first_faces,
         7,
         16384,
         in_specs=anywhere(4),
-        out_specs=whole(2),
-        out_shape=[vmem(6, width, depth)] * 2,
+        out_specs=whole(3),
+        out_shape=[vmem(6, width, depth)] * 2 + [vmem(8, depth)],
         scratch_shapes=[
             pltpu.VMEM((2, 19, width, 1, depth), F32),
             pltpu.VMEM((2, width, 1, depth), jnp.int32),
@@ -739,7 +751,7 @@
     post, flag, rate, edge, edge_flag, edge_rate = call(
         first_step,
         2,
-        in_specs=whole(3) + anywhere(2),
+        in_specs=whole(4),
         out_specs=whole(6),
         out_shape=[
             vmem(19, width + 2, length, depth),
@@ -749,8 +761,7 @@
             vmem(3, 4, length, depth),
             vmem(2, length, depth),
         ],
-        scratch_shapes=[pltpu.SMEM((4,), F32), pltpu.SemaphoreType.DMA],
-    )(*held(populations, fluid_mask, rate_class), given[3], far)
+    )(*held(populations, fluid_mask, rate_class, rates))
 
     far, near, halo, halo_flag, halo_edge, halo_flag_edge, halo_flag_last = call(
         join_sides,
@@ -761,7 +772,7 @@
         + [vmem(10, width, depth), vmem(6, width, depth)] * 2
         + [vmem(6, width, depth)],
         scratch_shapes=[pltpu.VMEM((2, 8, depth), F32)],
-    )(*held(edge, edge_flag, edge_rate, got_far, got_near))
+    )(*held(edge, edge_flag, edge_rate, got_near, got_far))
     got_far, got_near = exchange(far, near, "bx")
 
     final, sums, side, side_copy, own_flag, after_edge, last_flag = call(
@@ -782,10 +793,11 @@
             pltpu.VMEM((19, width, length, depth), F32),
             pltpu.VMEM((3, 19, 4, length, depth), F32),
             pltpu.SemaphoreType.DMA((3,)),
+            pltpu.SemaphoreType.DMA((4,)),
         ],
     )(*held(post, flag, rate, halo, halo_flag))
 
-    side_far, side_near, ends, ghost, came_flag, share = call(
+    side_near, side_far, ends, ghost, came_flag, share = call(
         second_faces,
         3,
         in_specs=whole(9),
@@ -819,7 +831,7 @@
     )(
         *main_memory(final),
         *held(ends, after_edge, last_flag, ghost, came_flag, halo_flag_last, side_copy, own_flag),
-        *held(side_far, side_near),
+        *held(side_near, side_far),
     )
     mean = call(
         mean_flow,

time: 45.5 us -> 43.9 us (0.965)
  waiting for transfers between devices: 3.14 us -> 6.73 us
  starting transfers between devices: 22.6 us -> 19.3 us
  Pallas kernels: 18.6 us -> 16.8 us
    ppermute x3, waiting for transfers between devices: 0.01 us -> 3.44 us  [exchange(): lax.ppermute(far, axis, far_pairs)]
    ppermute x3, starting transfers between devices: 5.3 us -> 2.65 us  [exchange(): lax.ppermute(near, axis, near_pairs)]
    pallas_call x1, Pallas kernels: 9.4 us -> 8.15 us  [body(): call(second_inner, 16, in_specs=whole(5), out_specs=anywhere(1) + whole(6...]
    ppermute x3, starting transfers between devices: 8.66 us -> 7.66 us  [exchange(): lax.ppermute(far, axis, far_pairs)]
    all_to_all x1, waiting for transfers between devices: 2.18 us -> 3.05 us  [body(): share = lax.all_to_all(share, ('bx', 'by'), 0, 0)]
    ppermute x3, waiting for transfers between devices: 0.95 us -> 0.24 us  [exchange(): lax.ppermute(near, axis, near_pairs)]
    pallas_call x2, Pallas kernels: 5.71 us -> 5.03 us  [the longest x1 3.63 us: body(): call(first_step, 2, in_specs=whole(4), out_specs=whole(6), out_shape=[vme...]
  transfers between devices with their start and end apart: 7 -> 7, of which waited for: 2 -> 3; matrix products, arithmetic and copies ran while one was open for 0% -> 0% of each run, Pallas kernels for 33% -> 30%
where the time goes in v3:
time: 43.9 us; the launch traced here: 43.8 us
  starting transfers between devices  19.3 us (44%)
  Pallas kernels  16.8 us (38%)
  waiting for transfers between devices  6.73 us (15%)
  between operations  0.74 us (2%)
    all_to_all x1, starting transfers between devices, body(): share = lax.all_to_all(share, ('bx', 'by'), 0, 0)  8.99 us
    pallas_call x1, Pallas kernels, body(): call(second_inner, 16, in_specs=whole(5), out_specs=anywhere(1) + whole(6...  8.15 us
    ppermute x3, starting transfers between devices, exchange(): lax.ppermute(far, axis, far_pairs)  7.66 us
    pallas_call x1, Pallas kernels, body(): call(first_step, 2, in_specs=whole(4), out_specs=whole(6), out_shape=[vme...  3.63 us
    ppermute x3, waiting for transfers between devices, exchange(): lax.ppermute(far, axis, far_pairs)  3.44 us
    all_to_all x1, waiting for transfers between devices, body(): share = lax.all_to_all(share, ('bx', 'by'), 0, 0)  3.05 us
    ppermute x3, starting transfers between devices, exchange(): lax.ppermute(near, axis, near_pairs)  2.65 us
    pallas_call x1, Pallas kernels, body(): call(last_faces, 6, in_specs=anywhere(1) + whole(10), out_specs=anywhere(...  1.48 us
  transfers between devices with their start and end apart: 7, of which 3 were waited for; matrix products, arithmetic and copies ran while one was open for 0% of the time, Pallas kernels for 30%

profile of v3, /device:TPU:1, one launch (start us, length us, event | category | flops | bytes accessed | tf_op | source)
XLA Modules:
  0.0 43.8 jit_solution(3391488435022184944)
XLA Ops:
  0.6 0.0 copy-start.2
  0.6 0.0 copy-start.1
  0.7 0.0 copy-start
  0.7 1.4 %first_faces.1 = (f32[6,32,128]{2,1,0:T(8,128)S(1)}, f32[6,32,128]{2,1,0:T(8,128)S(1)}, f32[8,128]{1,0:T(8,128)S(1)}) custom-call(f32[19,32,32,128]{3,2,1,0:T(8,128)} %f_ref.1, s32[32,32,128]{2,1,0:T(8,128)} %mask_ref.1, s32[32,32,128]{2,1,0:T(8,128)} %cls_ref.1, f32[4]{0:T(128)} %rates_hbm.1), custom_call_target="tpu_custom_call" | custom-call | bytes 16777216 | tf_op jit(solution)/shard_map/first_faces/pallas_call | solution.py:733
  2.1 1.5 %collective-permute-start = (f32[6,32,128]{2,1,0:T(8,128)S(1)}, f32[6,32,128]{2,1,0:T(8,128)S(1)}, u32[]{:S(2)}, u32[]{:S(2)}) collective-permute-start(f32[6,32,128]{2,1,0:T(8,128)S(1)} %get-tuple-element.38), channel_id=1, source_target_pairs={{0,1},{1,0},{2,3},{3,2},{4,5},{5,4},{6,7},{7,6},{8,9},{9,8},{10,11... | collective-permute-start | bytes 294920 | tf_op jit(solution)/shard_map/ppermute | solution.py:725
  3.6 1.3 %collective-permute-start.1 = (f32[6,32,128]{2,1,0:T(8,128)S(1)}, f32[6,32,128]{2,1,0:T(8,128)S(1)}, u32[]{:S(2)}, u32[]{:S(2)}) collective-permute-start(f32[6,32,128]{2,1,0:T(8,128)S(1)} %get-tuple-element.39), channel_id=1, source_target_pairs={{0,15},{1,2},{2,1},{3,4},{4,3},{5,6},{6,5},{7,8},{8,7},{9,10},{10,... | collective-permute-start | bytes 294920 | tf_op jit(solution)/shard_map/ppermute | solution.py:725
  4.8 0.0 copy-done.2
  4.9 0.0 copy-done.1
  4.9 0.2 copy-done
  5.1 3.6 %first_step.1 = (f32[19,34,32,128]{3,2,1,0:T(8,128)S(1)}, f32[3,34,32,128]{3,2,1,0:T(8,128)S(1)}, f32[32,32,128]{2,1,0:T(8,128)S(1)}, f32[19,4,32,128]{3,2,1,0:T...) custom-call(f32[19,32,32,128]{3,2,1,0:T(8,128)S(1)} %copy-done, s32[32,32,128]{2,1,0:T(8,128)S(1)} %copy-done.1, ...), custom_call_target="tpu_custom_call" | custom-call | tf_op jit(solution)/shard_map/first_step/pallas_call | solution.py:751
  8.7 0.0 collective-permute-done.near_ref
  8.7 0.0 collective-permute-done.1.far_ref
  8.7 0.2 join_sides.1
  9.0 5.7 %collective-permute-start.2 = (f32[17,32,128]{2,1,0:T(8,128)S(1)}, f32[17,32,128]{2,1,0:T(8,128)S(1)}, u32[]{:S(2)}, u32[]{:S(2)}) collective-permute-start(f32[17,32,128]{2,1,0:T(8,128)S(1)} %get-tuple-element.47), channel_id=1, source_target_pairs={{0,112},{16,32},{32,16},{48,64},{64,48},{80,96},{96,80},{112,0},{1... | collective-permute-start | bytes 835592 | tf_op jit(solution)/shard_map/ppermute | solution.py:725
  14.6 0.0 collective-permute-start.3
  14.6 8.2 %second_inner.1 = (f32[19,32,32,128]{3,2,1,0:T(8,128)}, f32[2,8,128]{2,1,0:T(8,128)S(1)}, f32[10,32,128]{2,1,0:T(8,128)S(1)}, f32[10,32,128]{2,1,0:T(8,128)S(1)}...) custom-call(f32[19,34,32,128]{3,2,1,0:T(8,128)S(1)} %get-tuple-element.32.post_ref, ...), custom_call_target="tpu_custom_call" | custom-call | tf_op jit(solution)/shard_map/second_inner/pallas_call | solution.py:778
  22.8 0.0 collective-permute-done.2.far_ref
  22.8 0.0 collective-permute-done.3.near_ref
  22.8 1.2 %second_faces.1 = (f32[5,40,128]{2,1,0:T(8,128)S(1)}, f32[5,40,128]{2,1,0:T(8,128)S(1)}, f32[19,2,32,128]{3,2,1,0:T(8,128)S(1)}, f32[5,2,32,128]{3,2,1,0:T(8,128...) custom-call(f32[19,4,32,128]{3,2,1,0:T(8,128)S(1)} %get-tuple-element.35.post_ref, ...), custom_call_target="tpu_custom_call" | custom-call | tf_op jit(solution)/shard_map/second_faces/pallas_call | solution.py:800
  24.1 9.0 %all-to-all-start = ((f32[128,2,128]{2,1,0:T(2,128)}), f32[128,2,128]{2,1,0:T(2,128)S(1)}, u32[]{:S(2)}, u32[]{:S(2)}) async-start(f32[128,2,128]{2,1,0:T(2,128)} %get-tuple-element.59), calls=%async_computation | async-start | bytes 262144 | tf_op jit(solution)/shard_map/all_to_all | solution.py:815
  33.1 1.1 %collective-permute-start.4 = (f32[5,40,128]{2,1,0:T(8,128)S(1)}, f32[5,40,128]{2,1,0:T(8,128)S(1)}, u32[]{:S(2)}, u32[]{:S(2)}) collective-permute-start(f32[5,40,128]{2,1,0:T(8,128)S(1)} %get-tuple-element.57), channel_id=1, source_target_pairs={{0,1},{1,0},{2,3},{3,2},{4,5},{5,4},{6,7},{7,6},{8,9},{9,8},{10,11... | collective-permute-start | bytes 307208 | tf_op jit(solution)/shard_map/ppermute | solution.py:725
  34.2 0.7 %collective-permute-start.5 = (f32[5,40,128]{2,1,0:T(8,128)S(1)}, f32[5,40,128]{2,1,0:T(8,128)S(1)}, u32[]{:S(2)}, u32[]{:S(2)}) collective-permute-start(f32[5,40,128]{2,1,0:T(8,128)S(1)} %get-tuple-element.58), channel_id=1, source_target_pairs={{0,15},{1,2},{2,1},{3,4},{4,3},{5,6},{6,5},{7,8},{8,7},{9,10},{10,... | collective-permute-start | bytes 307208 | tf_op jit(solution)/shard_map/ppermute | solution.py:725
  34.9 0.2 collective-permute-done.4.side_near
  35.2 3.4 %collective-permute-done.5.side_far = f32[5,40,128]{2,1,0:T(8,128)S(1)} collective-permute-done((f32[5,40,128]{2,1,0:T(8,128)S(1)}, f32[5,40,128]{2,1,0:T(8,128)S(1)}, u32[]{:S(2)}, u32[]{:S(2)}) %collective-permute-start.5) | collective-permute-done | bytes 102432 | tf_op jit(solution)/shard_map/ppermute | solution.py:725
  38.6 1.5 %last_faces.1.order_ref = f32[19,32,32,128]{3,2,1,0:T(8,128)} custom-call(f32[19,32,32,128]{3,2,1,0:T(8,128)} %get-tuple-element.42.out_in, f32[19,2,32,128]{3,2,1,0:T(8,128)S(1)} %get-tuple-element.49.ends_ref, f32[19,4,32,128]{3,2,1,0:T(8,128)S(1)} %get-tuple-element.50.edge_ref, ...), custom_call_target="tpu_custom_call", output_to_operand_aliasing={{}: (0, {})} | custom-call | tf_op jit(solution)/shard_map/last_faces/pallas_call | solution.py:817
  40.1 3.1 %all-to-all-done.share_ref = f32[128,2,128]{2,1,0:T(2,128)S(1)} async-done(((f32[128,2,128]{2,1,0:T(2,128)}), f32[128,2,128]{2,1,0:T(2,128)S(1)}, u32[]{:S(2)}, u32[]{:S(2)}) %all-to-all-start) | async-done | bytes 131104 | tf_op jit(solution)/shard_map/all_to_all | solution.py:815
  43.1 0.6 %mean_flow.1 = f32[1,128]{1,0:T(1,128)} custom-call(f32[128,2,128]{2,1,0:T(2,128)S(1)} %all-to-all-done.share_ref, f32[19,32,32,128]{3,2,1,0:T(8,128)} %last_faces.1.order_ref), custom_call_target="tpu_custom_call" | custom-call | tf_op jit(solution)/shard_map/mean_flow/pallas_call | solution.py:836
Async XLA Ops:
  0.6 4.2 %copy-start.2 = (s32[32,32,128]{2,1,0:T(8,128)S(1)}, s32[32,32,128]{2,1,0:T(8,128)}, u32[]{:S(2)}) copy-start(s32[32,32,128]{2,1,0:T(8,128)} %cls_ref.1) | copy-start | bytes 1572868
  0.6 4.2 %copy-start.1 = (s32[32,32,128]{2,1,0:T(8,128)S(1)}, s32[32,32,128]{2,1,0:T(8,128)}, u32[]{:S(2)}) copy-start(s32[32,32,128]{2,1,0:T(8,128)} %mask_ref.1) | copy-start | bytes 1572868
  0.7 4.4 %copy-start = (f32[19,32,32,128]{3,2,1,0:T(8,128)S(1)}, f32[19,32,32,128]{3,2,1,0:T(8,128)}, u32[]{:S(2)}) copy-start(f32[19,32,32,128]{3,2,1,0:T(8,128)} %f_ref.1) | copy-start | bytes 29884420
  2.1 6.6 %collective-permute-start = (f32[6,32,128]{2,1,0:T(8,128)S(1)}, f32[6,32,128]{2,1,0:T(8,128)S(1)}, u32[]{:S(2)}, u32[]{:S(2)}) collective-permute-start(f32[6,32,128]{2,1,0:T(8,128)S(1)} %get-tuple-element.38), channel_id=1, source_target_pairs={{0,1},{1,0},{2,3},{3,2},{4,5},{5,4},{6,7},{7,6},{8,9},{9,8},{10,11... | collective-permute-start | bytes 294920 | tf_op jit(solution)/shard_map/ppermute | solution.py:725
  3.6 5.2 %collective-permute-start.1 = (f32[6,32,128]{2,1,0:T(8,128)S(1)}, f32[6,32,128]{2,1,0:T(8,128)S(1)}, u32[]{:S(2)}, u32[]{:S(2)}) collective-permute-start(f32[6,32,128]{2,1,0:T(8,128)S(1)} %get-tuple-element.39), channel_id=1, source_target_pairs={{0,15},{1,2},{2,1},{3,4},{4,3},{5,6},{6,5},{7,8},{8,7},{9,10},{10,... | collective-permute-start | bytes 294920 | tf_op jit(solution)/shard_map/ppermute | solution.py:725
  9.0 13.8 %collective-permute-start.2 = (f32[17,32,128]{2,1,0:T(8,128)S(1)}, f32[17,32,128]{2,1,0:T(8,128)S(1)}, u32[]{:S(2)}, u32[]{:S(2)}) collective-permute-start(f32[17,32,128]{2,1,0:T(8,128)S(1)} %get-tuple-element.47), channel_id=1, source_target_pairs={{0,112},{16,32},{32,16},{48,64},{64,48},{80,96},{96,80},{112,0},{1... | collective-permute-start | bytes 835592 | tf_op jit(solution)/shard_map/ppermute | solution.py:725
  14.6 8.2 %collective-permute-start.3 = (f32[17,32,128]{2,1,0:T(8,128)S(1)}, f32[17,32,128]{2,1,0:T(8,128)S(1)}, u32[]{:S(2)}, u32[]{:S(2)}) collective-permute-start(f32[17,32,128]{2,1,0:T(8,128)S(1)} %get-tuple-element.48), channel_id=1, source_target_pairs={{0,16},{16,0},{32,48},{48,32},{64,80},{80,64},{96,112},{112,96},{1... | collective-permute-start | bytes 835592 | tf_op jit(solution)/shard_map/ppermute | solution.py:725
  24.1 19.1 %all-to-all-start = ((f32[128,2,128]{2,1,0:T(2,128)}), f32[128,2,128]{2,1,0:T(2,128)S(1)}, u32[]{:S(2)}, u32[]{:S(2)}) async-start(f32[128,2,128]{2,1,0:T(2,128)} %get-tuple-element.59), calls=%async_computation | async-start | bytes 262144 | tf_op jit(solution)/shard_map/all_to_all | solution.py:815
  33.1 2.1 %collective-permute-start.4 = (f32[5,40,128]{2,1,0:T(8,128)S(1)}, f32[5,40,128]{2,1,0:T(8,128)S(1)}, u32[]{:S(2)}, u32[]{:S(2)}) collective-permute-start(f32[5,40,128]{2,1,0:T(8,128)S(1)} %get-tuple-element.57), channel_id=1, source_target_pairs={{0,1},{1,0},{2,3},{3,2},{4,5},{5,4},{6,7},{7,6},{8,9},{9,8},{10,11... | collective-permute-start | bytes 307208 | tf_op jit(solution)/shard_map/ppermute | solution.py:725
  34.2 4.4 %collective-permute-start.5 = (f32[5,40,128]{2,1,0:T(8,128)S(1)}, f32[5,40,128]{2,1,0:T(8,128)S(1)}, u32[]{:S(2)}, u32[]{:S(2)}) collective-permute-start(f32[5,40,128]{2,1,0:T(8,128)S(1)} %get-tuple-element.58), channel_id=1, source_target_pairs={{0,15},{1,2},{2,1},{3,4},{4,3},{5,6},{6,5},{7,8},{8,7},{9,10},{10,... | collective-permute-start | bytes 307208 | tf_op jit(solution)/shard_map/ppermute | solution.py:725

commit v4 on v3

--- a/solution.py
+++ b/solution.py
@@ -32,6 +32,7 @@
 UP_Y = [q for q in range(19) if VELOCITY[q][1] == 1]
 DOWN_Y = [OPPOSITE[q] for q in UP_Y]
 FLAG, NEXT, SUMS, RATE, ROWS = 5, 6, 11, 15, 16
+GROUPS = 4
 F32 = jnp.float32
 MIB = 1024 * 1024
 
@@ -57,25 +58,27 @@
 
 
 def relax(f, rho, mx, my, mz, rate):
-    inv = 4.5 / rho
-    ux = inv * mx
-    uy = inv * my
-    uz = inv * mz
-    tx = ux * mx
-    ty = uy * my
-    tz = uz * mz
-    base = rho - ((tx + ty) + tz) * (1.0 / 3.0)
+    r36 = rate * (1.0 / 36.0)
+    scale = r36 * (4.5 / rho)
+    vx = scale * mx
+    vy = scale * my
+    vz = scale * mz
+    tx = vx * mx
+    ty = vy * my
+    tz = vz * mz
+    base = r36 * rho - ((tx + ty) + tz) * (1.0 / 3.0)
     keep = 1.0 - rate
-    r36 = rate * (1.0 / 36.0)
-    r18 = rate * (1.0 / 18.0)
     r12 = rate * (1.0 / 12.0)
     gx = r12 * mx
     gy = r12 * my
     gz = r12 * mz
-    ux2 = ux + ux
-    uy2 = uy + uy
-    cross = {7: ux2 * my, 11: ux2 * mz, 15: uy2 * mz}
-    pair_base = {7: base + (tx + ty), 11: base + (tx + tz), 15: base + (ty + tz)}
+    vx2 = vx + vx
+    vy2 = vy + vy
+    cross = {7: vx2 * my, 11: vx2 * mz, 15: vy2 * mz}
+    bx = base + tx
+    by = base + ty
+    bz = base + tz
+    pair_base = {7: bx + ty, 11: bx + tz, 15: by + tz}
     lean = {7: (gx, gy), 11: (gx, gz), 15: (gy, gz)}
     out = [None] * 19
 
@@ -86,13 +89,13 @@
             out[q + 1] = keep * f[q + 1] + (even - odd)
 
     if f[0] is not None:
-        out[0] = keep * f[0] + (rate * (1.0 / 3.0)) * base
-    for q, t, g in ((1, tx, gx), (3, ty, gy), (5, tz, gz)):
-        put(q, r18 * (base + t), g + g)
+        out[0] = keep * f[0] + 12.0 * base
+    for q, b, g in ((1, bx, gx), (3, by, gy), (5, bz, gz)):
+        put(q, b + b, g + g)
     for q in (7, 11, 15):
         one, two = lean[q]
-        put(q, r36 * (pair_base[q] + cross[q]), one + two)
-        put(q + 2, r36 * (pair_base[q] - cross[q]), one - two)
+        put(q, pair_base[q] + cross[q], one + two)
+        put(q + 2, pair_base[q] - cross[q], one - two)
     return out
 
 
@@ -151,7 +154,7 @@
 
 
 def shifted(ref, k, plane, g, cy, low=None, high=None, spare=False, step=0):
-    groups = ref.shape[2] // 8
+    groups = GROUPS
     if cy == 1 and g == 0:
         value = beyond(ref, k, plane, g, cy, spare)
         if low is not None:
@@ -401,10 +404,10 @@
         return carry
 
     zero = jnp.zeros((8, 128), F32)
-    carry = lax.fori_loop(1, 4, first, (zero, zero))
+    carry = lax.fori_loop(1, 4, first, (zero, zero), unroll=3)
     parts = (width - 4) // chunk
 
-    def part(c, carry, steps=chunk):
+    def part(c, carry):
         slot = lax.rem(c, slots)
 
         @pl.when(c >= slots)
@@ -419,9 +422,8 @@
                 carry = collide_tile(x + 2, g, carry)
             return carry
 
-        carry = lax.fori_loop(0, steps, step, carry, unroll=steps if steps == chunk else 1)
-        if steps == chunk:
-            copy_out(c).start()
+        carry = lax.fori_loop(0, chunk, step, carry, unroll=chunk)
+        copy_out(c).start()
         return carry
 
     carry = lax.fori_loop(0, parts - 1, part, carry)
@@ -435,26 +437,34 @@
             last_sems.at[j],
         )
 
-    flux, count = part(parts - 1, carry, chunk - 1)
-    copy_last(0, chunk - 1).start()
-    for g in range(groups):
-        stream_tile(last_x + chunk - 1, g, last_slot, chunk - 1)
-    copy_last(chunk - 1, 1).start()
+    @pl.when(parts > slots)
+    def _():
+        copy_out(parts - 1 - slots).wait()
+
+    for j in range(chunk):
+        x = last_x + j
+        for g in range(groups):
+            stream_tile(x, g, last_slot, j)
+        copy_last(j, 1).start()
+        for g in range(groups if j < chunk - 1 else 0):
+            carry = collide_tile(x + 2, g, carry)
+    flux, count = carry
     sums_ref[0] = flux
     sums_ref[1] = count
-    flat = next_ref.reshape(19, width * length, 128)
-    flags = flag_ref.reshape(3, (width + 2) * length, 128)
+    pitch = next_ref.shape[2]
+    flat = next_ref.reshape(19, width * pitch, 128)
+    flags = flag_ref.reshape(3, (width + 2) * pitch, 128)
     for g in range(width // 8):
-        low_at = pl.ds(g * 8 * length, 8, stride=length)
-        high_at = pl.ds(g * 8 * length + length - 1, 8, stride=length)
+        low_at = pl.ds(g * 8 * pitch, 8, stride=pitch)
+        high_at = pl.ds(g * 8 * pitch + length - 1, 8, stride=pitch)
         for k in range(5):
             low = flat[DOWN_Y[k], low_at, :]
             high = flat[UP_Y[k], high_at, :]
             for to_ref in (side_ref, side_copy):
                 to_ref[k, tile(g), :] = low
                 to_ref[5 + k, tile(g), :] = high
-        own_flag[0, tile(g), :] = flags[1, pl.ds((g * 8 + 1) * length, 8, stride=length), :]
-        own_flag[1, tile(g), :] = flags[1, pl.ds((g * 8 + 2) * length - 1, 8, stride=length), :]
+        own_flag[0, tile(g), :] = flags[1, pl.ds((g * 8 + 1) * pitch, 8, stride=pitch), :]
+        own_flag[1, tile(g), :] = flags[1, pl.ds((g * 8 + 1) * pitch + length - 1, 8, stride=pitch), :]
     for e, x in enumerate((1, 2, width - 3, width - 2)):
         for g in range(groups):
             for q in range(19):
@@ -465,8 +475,8 @@
                 edge_flag[s, e, tile(g), :] = flag_ref[s, x + 1, tile(g), :]
     for c in range(parts - slots, parts - 1):
         copy_out(c).wait()
-    copy_last(0, chunk - 1).wait()
-    copy_last(chunk - 1, 1).wait()
+    for j in range(chunk):
+        copy_last(j, 1).wait()
 
 
 def second_faces(
@@ -754,8 +764,8 @@
         in_specs=whole(4),
         out_specs=whole(6),
         out_shape=[
-            vmem(19, width + 2, length, depth),
-            vmem(3, width + 2, length, depth),
+            vmem(19, width + 2, length + 8, depth),
+            vmem(3, width + 2, length + 8, depth),
             vmem(width, length, depth),
             vmem(19, 4, length, depth),
             vmem(3, 4, length, depth),
@@ -777,7 +787,7 @@
 
     final, sums, side, side_copy, own_flag, after_edge, last_flag = call(
         second_inner,
-        16,
+        20,
         in_specs=whole(5),
         out_specs=anywhere(1) + whole(6),
         out_shape=[
@@ -790,7 +800,7 @@
             vmem(3, 6, length, depth),
         ],
         scratch_shapes=[
-            pltpu.VMEM((19, width, length, depth), F32),
+            pltpu.VMEM((19, width, length + 8, depth), F32),
             pltpu.VMEM((3, 19, 4, length, depth), F32),
             pltpu.SemaphoreType.DMA((3,)),
             pltpu.SemaphoreType.DMA((4,)),

time: 43.9 us -> 43.5 us (level)
  Pallas kernels: 16.8 us -> 16 us
  transfers between devices with their start and end apart: 7 -> 7, of which waited for: 3 -> 3; matrix products, arithmetic and copies ran while one was open for 0% -> 0% of each run, Pallas kernels for 30% -> 29%
where the time goes in v4:
time: 43.5 us; the launch traced here: 43.3 us
  starting transfers between devices  19.6 us (45%)
  Pallas kernels  16 us (37%)
  waiting for transfers between devices  6.73 us (15%)
  between operations  0.74 us (2%)
    all_to_all x1, starting transfers between devices, body(): share = lax.all_to_all(share, ('bx', 'by'), 0, 0)  9.33 us
    pallas_call x1, Pallas kernels, body(): call(second_inner, 20, in_specs=whole(5), out_specs=anywhere(1) + whole(6...  7.75 us
    ppermute x3, starting transfers between devices, exchange(): lax.ppermute(far, axis, far_pairs)  7.66 us
    ppermute x3, waiting for transfers between devices, exchange(): lax.ppermute(far, axis, far_pairs)  3.44 us
    pallas_call x1, Pallas kernels, body(): call(first_step, 2, in_specs=whole(4), out_specs=whole(6), out_shape=[vme...  3.29 us
    all_to_all x1, waiting for transfers between devices, body(): share = lax.all_to_all(share, ('bx', 'by'), 0, 0)  3.05 us
    ppermute x3, starting transfers between devices, exchange(): lax.ppermute(near, axis, near_pairs)  2.65 us
    pallas_call x1, Pallas kernels, body(): call(last_faces, 6, in_specs=anywhere(1) + whole(10), out_specs=anywhere(...  1.48 us
  transfers between devices with their start and end apart: 7, of which 3 were waited for; matrix products, arithmetic and copies ran while one was open for 0% of the time, Pallas kernels for 29%

profile of v4, /device:TPU:1, one launch (start us, length us, event | category | flops | bytes accessed | tf_op | source)
XLA Modules:
  0.0 43.3 jit_solution(4657634882564885360)
XLA Ops:
  0.6 0.0 copy-start.2
  0.6 0.0 copy-start.1
  0.7 0.0 copy-start
  0.7 1.4 %first_faces.1 = (f32[6,32,128]{2,1,0:T(8,128)S(1)}, f32[6,32,128]{2,1,0:T(8,128)S(1)}, f32[8,128]{1,0:T(8,128)S(1)}) custom-call(f32[19,32,32,128]{3,2,1,0:T(8,128)} %f_ref.1, s32[32,32,128]{2,1,0:T(8,128)} %mask_ref.1, s32[32,32,128]{2,1,0:T(8,128)} %cls_ref.1, f32[4]{0:T(128)} %rates_hbm.1), custom_call_target="tpu_custom_call" | custom-call | bytes 16777216 | tf_op jit(solution)/shard_map/first_faces/pallas_call | solution.py:743
  2.1 1.5 %collective-permute-start = (f32[6,32,128]{2,1,0:T(8,128)S(1)}, f32[6,32,128]{2,1,0:T(8,128)S(1)}, u32[]{:S(2)}, u32[]{:S(2)}) collective-permute-start(f32[6,32,128]{2,1,0:T(8,128)S(1)} %get-tuple-element.38), channel_id=1, source_target_pairs={{0,1},{1,0},{2,3},{3,2},{4,5},{5,4},{6,7},{7,6},{8,9},{9,8},{10,11... | collective-permute-start | bytes 294920 | tf_op jit(solution)/shard_map/ppermute | solution.py:735
  3.6 1.3 %collective-permute-start.1 = (f32[6,32,128]{2,1,0:T(8,128)S(1)}, f32[6,32,128]{2,1,0:T(8,128)S(1)}, u32[]{:S(2)}, u32[]{:S(2)}) collective-permute-start(f32[6,32,128]{2,1,0:T(8,128)S(1)} %get-tuple-element.39), channel_id=1, source_target_pairs={{0,15},{1,2},{2,1},{3,4},{4,3},{5,6},{6,5},{7,8},{8,7},{9,10},{10,... | collective-permute-start | bytes 294920 | tf_op jit(solution)/shard_map/ppermute | solution.py:735
  4.8 0.0 copy-done.2
  4.9 0.0 copy-done.1
  4.9 0.2 copy-done
  5.1 3.3 %first_step.1 = (f32[19,34,40,128]{3,2,1,0:T(8,128)S(1)}, f32[3,34,40,128]{3,2,1,0:T(8,128)S(1)}, f32[32,32,128]{2,1,0:T(8,128)S(1)}, f32[19,4,32,128]{3,2,1,0:T...) custom-call(f32[19,32,32,128]{3,2,1,0:T(8,128)S(1)} %copy-done, s32[32,32,128]{2,1,0:T(8,128)S(1)} %copy-done.1, ...), custom_call_target="tpu_custom_call" | custom-call | tf_op jit(solution)/shard_map/first_step/pallas_call | solution.py:761
  8.4 0.0 collective-permute-done.near_ref
  8.4 0.0 collective-permute-done.1.far_ref
  8.4 0.2 join_sides.1
  8.6 5.7 %collective-permute-start.2 = (f32[17,32,128]{2,1,0:T(8,128)S(1)}, f32[17,32,128]{2,1,0:T(8,128)S(1)}, u32[]{:S(2)}, u32[]{:S(2)}) collective-permute-start(f32[17,32,128]{2,1,0:T(8,128)S(1)} %get-tuple-element.47), channel_id=1, source_target_pairs={{0,112},{16,32},{32,16},{48,64},{64,48},{80,96},{96,80},{112,0},{1... | collective-permute-start | bytes 835592 | tf_op jit(solution)/shard_map/ppermute | solution.py:735
  14.3 0.0 collective-permute-start.3
  14.3 7.7 %second_inner.1 = (f32[19,32,32,128]{3,2,1,0:T(8,128)}, f32[2,8,128]{2,1,0:T(8,128)S(1)}, f32[10,32,128]{2,1,0:T(8,128)S(1)}, f32[10,32,128]{2,1,0:T(8,128)S(1)}...) custom-call(f32[19,34,40,128]{3,2,1,0:T(8,128)S(1)} %get-tuple-element.32.post_ref, ...), custom_call_target="tpu_custom_call" | custom-call | tf_op jit(solution)/shard_map/second_inner/pallas_call | solution.py:788
  22.1 0.0 collective-permute-done.2.far_ref
  22.1 0.0 collective-permute-done.3.near_ref
  22.1 1.2 %second_faces.1 = (f32[5,40,128]{2,1,0:T(8,128)S(1)}, f32[5,40,128]{2,1,0:T(8,128)S(1)}, f32[19,2,32,128]{3,2,1,0:T(8,128)S(1)}, f32[5,2,32,128]{3,2,1,0:T(8,128...) custom-call(f32[19,4,32,128]{3,2,1,0:T(8,128)S(1)} %get-tuple-element.35.post_ref, ...), custom_call_target="tpu_custom_call" | custom-call | tf_op jit(solution)/shard_map/second_faces/pallas_call | solution.py:810
  23.3 9.3 %all-to-all-start = ((f32[128,2,128]{2,1,0:T(2,128)}), f32[128,2,128]{2,1,0:T(2,128)S(1)}, u32[]{:S(2)}, u32[]{:S(2)}) async-start(f32[128,2,128]{2,1,0:T(2,128)} %get-tuple-element.59), calls=%async_computation | async-start | bytes 262144 | tf_op jit(solution)/shard_map/all_to_all | solution.py:825
  32.6 1.1 %collective-permute-start.4 = (f32[5,40,128]{2,1,0:T(8,128)S(1)}, f32[5,40,128]{2,1,0:T(8,128)S(1)}, u32[]{:S(2)}, u32[]{:S(2)}) collective-permute-start(f32[5,40,128]{2,1,0:T(8,128)S(1)} %get-tuple-element.57), channel_id=1, source_target_pairs={{0,1},{1,0},{2,3},{3,2},{4,5},{5,4},{6,7},{7,6},{8,9},{9,8},{10,11... | collective-permute-start | bytes 307208 | tf_op jit(solution)/shard_map/ppermute | solution.py:735
  33.8 0.7 %collective-permute-start.5 = (f32[5,40,128]{2,1,0:T(8,128)S(1)}, f32[5,40,128]{2,1,0:T(8,128)S(1)}, u32[]{:S(2)}, u32[]{:S(2)}) collective-permute-start(f32[5,40,128]{2,1,0:T(8,128)S(1)} %get-tuple-element.58), channel_id=1, source_target_pairs={{0,15},{1,2},{2,1},{3,4},{4,3},{5,6},{6,5},{7,8},{8,7},{9,10},{10,... | collective-permute-start | bytes 307208 | tf_op jit(solution)/shard_map/ppermute | solution.py:735
  34.5 0.2 collective-permute-done.4.side_near
  34.7 3.4 %collective-permute-done.5.side_far = f32[5,40,128]{2,1,0:T(8,128)S(1)} collective-permute-done((f32[5,40,128]{2,1,0:T(8,128)S(1)}, f32[5,40,128]{2,1,0:T(8,128)S(1)}, u32[]{:S(2)}, u32[]{:S(2)}) %collective-permute-start.5) | collective-permute-done | bytes 102432 | tf_op jit(solution)/shard_map/ppermute | solution.py:735
  38.2 1.5 %last_faces.1.order_ref = f32[19,32,32,128]{3,2,1,0:T(8,128)} custom-call(f32[19,32,32,128]{3,2,1,0:T(8,128)} %get-tuple-element.42.out_in, f32[19,2,32,128]{3,2,1,0:T(8,128)S(1)} %get-tuple-element.49.ends_ref, f32[19,4,32,128]{3,2,1,0:T(8,128)S(1)} %get-tuple-element.50.edge_ref, ...), custom_call_target="tpu_custom_call", output_to_operand_aliasing={{}: (0, {})} | custom-call | tf_op jit(solution)/shard_map/last_faces/pallas_call | solution.py:827
  39.7 3.1 %all-to-all-done.share_ref = f32[128,2,128]{2,1,0:T(2,128)S(1)} async-done(((f32[128,2,128]{2,1,0:T(2,128)}), f32[128,2,128]{2,1,0:T(2,128)S(1)}, u32[]{:S(2)}, u32[]{:S(2)}) %all-to-all-start) | async-done | bytes 131104 | tf_op jit(solution)/shard_map/all_to_all | solution.py:825
  42.7 0.6 %mean_flow.1 = f32[1,128]{1,0:T(1,128)} custom-call(f32[128,2,128]{2,1,0:T(2,128)S(1)} %all-to-all-done.share_ref, f32[19,32,32,128]{3,2,1,0:T(8,128)} %last_faces.1.order_ref), custom_call_target="tpu_custom_call" | custom-call | tf_op jit(solution)/shard_map/mean_flow/pallas_call | solution.py:846
Async XLA Ops:
  0.6 4.2 %copy-start.2 = (s32[32,32,128]{2,1,0:T(8,128)S(1)}, s32[32,32,128]{2,1,0:T(8,128)}, u32[]{:S(2)}) copy-start(s32[32,32,128]{2,1,0:T(8,128)} %cls_ref.1) | copy-start | bytes 1572868
  0.6 4.2 %copy-start.1 = (s32[32,32,128]{2,1,0:T(8,128)S(1)}, s32[32,32,128]{2,1,0:T(8,128)}, u32[]{:S(2)}) copy-start(s32[32,32,128]{2,1,0:T(8,128)} %mask_ref.1) | copy-start | bytes 1572868
  0.7 4.4 %copy-start = (f32[19,32,32,128]{3,2,1,0:T(8,128)S(1)}, f32[19,32,32,128]{3,2,1,0:T(8,128)}, u32[]{:S(2)}) copy-start(f32[19,32,32,128]{3,2,1,0:T(8,128)} %f_ref.1) | copy-start | bytes 29884420
  2.1 6.3 %collective-permute-start = (f32[6,32,128]{2,1,0:T(8,128)S(1)}, f32[6,32,128]{2,1,0:T(8,128)S(1)}, u32[]{:S(2)}, u32[]{:S(2)}) collective-permute-start(f32[6,32,128]{2,1,0:T(8,128)S(1)} %get-tuple-element.38), channel_id=1, source_target_pairs={{0,1},{1,0},{2,3},{3,2},{4,5},{5,4},{6,7},{7,6},{8,9},{9,8},{10,11... | collective-permute-start | bytes 294920 | tf_op jit(solution)/shard_map/ppermute | solution.py:735
  3.6 4.8 %collective-permute-start.1 = (f32[6,32,128]{2,1,0:T(8,128)S(1)}, f32[6,32,128]{2,1,0:T(8,128)S(1)}, u32[]{:S(2)}, u32[]{:S(2)}) collective-permute-start(f32[6,32,128]{2,1,0:T(8,128)S(1)} %get-tuple-element.39), channel_id=1, source_target_pairs={{0,15},{1,2},{2,1},{3,4},{4,3},{5,6},{6,5},{7,8},{8,7},{9,10},{10,... | collective-permute-start | bytes 294920 | tf_op jit(solution)/shard_map/ppermute | solution.py:735
  8.6 13.4 %collective-permute-start.2 = (f32[17,32,128]{2,1,0:T(8,128)S(1)}, f32[17,32,128]{2,1,0:T(8,128)S(1)}, u32[]{:S(2)}, u32[]{:S(2)}) collective-permute-start(f32[17,32,128]{2,1,0:T(8,128)S(1)} %get-tuple-element.47), channel_id=1, source_target_pairs={{0,112},{16,32},{32,16},{48,64},{64,48},{80,96},{96,80},{112,0},{1... | collective-permute-start | bytes 835592 | tf_op jit(solution)/shard_map/ppermute | solution.py:735
  14.3 7.8 %collective-permute-start.3 = (f32[17,32,128]{2,1,0:T(8,128)S(1)}, f32[17,32,128]{2,1,0:T(8,128)S(1)}, u32[]{:S(2)}, u32[]{:S(2)}) collective-permute-start(f32[17,32,128]{2,1,0:T(8,128)S(1)} %get-tuple-element.48), channel_id=1, source_target_pairs={{0,16},{16,0},{32,48},{48,32},{64,80},{80,64},{96,112},{112,96},{1... | collective-permute-start | bytes 835592 | tf_op jit(solution)/shard_map/ppermute | solution.py:735
  23.3 19.4 %all-to-all-start = ((f32[128,2,128]{2,1,0:T(2,128)}), f32[128,2,128]{2,1,0:T(2,128)S(1)}, u32[]{:S(2)}, u32[]{:S(2)}) async-start(f32[128,2,128]{2,1,0:T(2,128)} %get-tuple-element.59), calls=%async_computation | async-start | bytes 262144 | tf_op jit(solution)/shard_map/all_to_all | solution.py:825
  32.6 2.1 %collective-permute-start.4 = (f32[5,40,128]{2,1,0:T(8,128)S(1)}, f32[5,40,128]{2,1,0:T(8,128)S(1)}, u32[]{:S(2)}, u32[]{:S(2)}) collective-permute-start(f32[5,40,128]{2,1,0:T(8,128)S(1)} %get-tuple-element.57), channel_id=1, source_target_pairs={{0,1},{1,0},{2,3},{3,2},{4,5},{5,4},{6,7},{7,6},{8,9},{9,8},{10,11... | collective-permute-start | bytes 307208 | tf_op jit(solution)/shard_map/ppermute | solution.py:735
  33.8 4.4 %collective-permute-start.5 = (f32[5,40,128]{2,1,0:T(8,128)S(1)}, f32[5,40,128]{2,1,0:T(8,128)S(1)}, u32[]{:S(2)}, u32[]{:S(2)}) collective-permute-start(f32[5,40,128]{2,1,0:T(8,128)S(1)} %get-tuple-element.58), channel_id=1, source_target_pairs={{0,15},{1,2},{2,1},{3,4},{4,3},{5,6},{6,5},{7,8},{8,7},{9,10},{10,... | collective-permute-start | bytes 307208 | tf_op jit(solution)/shard_map/ppermute | solution.py:735
